TPU v7x, 128 devices: a whole 4x4x4 slice. The times are simulated.
128 devices in a mesh: tm: 32 (over x, y, core), grp: 4 (over z).
Axes of the slice: x: 4, y: 4, z: 4, core: 2. Of those that a mesh axis runs over, the one named last changes fastest.
Arguments:
- init_field: float32 [256, 256], replicated, may hold values from -3 to 3
- reaction: float32 [256, 256], replicated, may hold values from 0.0003 to 0.0015
- guesses: float32 [128, 256, 256], P(('tm', 'grp')), may hold values from -3 to 3
Outputs:
- c_points: float32 [128, 256, 256], P(('tm', 'grp'))
- corners: float32 [32, 256, 256], P('tm')
All inputs are finite; a program needn't handle non-finite values.
Results may differ from a plain program's by a relative error of at most 0.00002.
Values sent between devices are 32-bit elements; how exact they have to be, the bound alone decides.
A program may use at most 64 MiB of HBM per device.

v0:
```python
import jax
import jax.numpy as jnp
from jax import lax
from jax.sharding import PartitionSpec as P

STEPS = 16


KAPPA = 0.0035


def passed_along(block, axis, distance):
    devices = range(lax.axis_size(axis))
    route = [(i - distance, i) for i in devices if i - distance in devices]
    return lax.ppermute(block, axis, route)


def advance(values, reaction, factor):
    beside = (
        jnp.roll(values, 1, -2)
        + jnp.roll(values, -1, -2)
        + jnp.roll(values, 1, -1)
        + jnp.roll(values, -1, -1)
    )
    return values + factor * (
        KAPPA * (beside - 4.0 * values) + reaction * (values - values * values * values)
    )


def repeat(values, reaction, factor, count):
    return lax.fori_loop(0, count, lambda index, state: advance(state, reaction, factor), values)


def coarse_solve(init_field, reaction, coarse_term, group_index, factor):

    def one_turn(counter, carried):
        incoming = passed_along(carried[1], "tm", 1)
        incoming = jnp.where(group_index == 0, init_field, incoming)
        return (incoming, advance(incoming, reaction, factor) + coarse_term)

    return lax.fori_loop(0, lax.axis_size("tm"), one_turn, (init_field, jnp.zeros_like(init_field)))


def local(init_field, reaction, guesses):
    members = lax.axis_size("grp")
    member = lax.axis_index("grp")
    group_index = lax.axis_index("tm")
    position = group_index * members + member
    fine_factor = float(STEPS)
    coarse_factor = float(STEPS * members)
    earlier = jnp.where(position == 0, init_field, guesses[0])
    relaxed = repeat(earlier, reaction, 1.0, STEPS)
    start = passed_along(relaxed, ("tm", "grp"), 1)
    start = jnp.where(position == 0, init_field, start)
    term = repeat(start, reaction, 1.0, STEPS) - advance(start, reaction, fine_factor)
    terms, ends = (
        lax.all_gather(term[None], "grp", axis=0, tiled=True),
        lax.all_gather(relaxed[None], "grp", axis=0, tiled=True),
    )
    corner = passed_along(ends[members - 1], "tm", 1)
    corner = jnp.where(group_index == 0, init_field, corner)
    for index in range(members):
        corner = advance(corner, reaction, fine_factor) + terms[index]
    fresh = passed_along(corner, "tm", 1)
    fresh = jnp.where(group_index == 0, init_field, fresh)
    composed = fresh
    for index in range(members):
        composed = advance(composed, reaction, fine_factor) + terms[index]
    coarse_term = composed - advance(fresh, reaction, coarse_factor)
    before, after = coarse_solve(init_field, reaction, coarse_term, group_index, coarse_factor)
    result = after
    carried = before
    for index in range(members - 1):
        carried = advance(carried, reaction, fine_factor) + terms[index]
        result = jnp.where(member == index, carried, result)
    return (result[None], corner[None])


def solution(mesh):
    return jax.shard_map(
        local,
        mesh=mesh,
        in_specs=(P(), P(), P(("tm", "grp"), None, None)),
        out_specs=(P(("tm", "grp"), None, None), P("tm", None, None)),
        check_vma=False,
    )
```

profile of v0, /device:TPU:5, one launch (start us, length us, event | category | flops | bytes accessed | tf_op | source)
XLA Modules:
  0.0 454.0 jit_solution(7764846863122176748)
XLA Ops:
  8.3 9.1 %while.35 = (s32[]{:T(128)}, f32[256,256]{1,0:T(8,128)S(1)}, f32[256,256]{1,0:T(8,128)S(1)}, s32[]{:T(128)}) while((s32[]{:T(128)}, f32[256,256]{1,0:T(8,128)S(1)}, f32[256,256]{1,0:T(8,128)S(1)}, s32[]{:T(128)}) %tuple.158), condition=%wide.region_1.2_spmd, body=%wide.region_0.1_spmd.sunk | while | flops 1048578 | bytes 3932213 | solution.py:31
  18.2 3.7 collective-permute-start.2
  21.9 22.0 %all-gather.5.cloned.1.call-done = f32[1024,256]{1,0:T(8,128)} async-done(((f32[256,256]{1,0:T(8,128)}), f32[1024,256]{1,0:T(8,128)}) %all-gather.5.cloned.1.call-update) | async-done | bytes 1048592 | tf_op jit(solution)/shard_map/all_gather | solution.py:58
  44.9 4.6 %collective-permute-start.1 = (f32[256,256]{1,0:T(8,128)S(1)}, f32[256,256]{1,0:T(8,128)S(1)}, u32[]{:S(2)}, u32[]{:S(2)}) collective-permute-start(f32[256,256]{1,0:T(8,128)S(1)} %slice.536), channel_id=1, source_target_pairs={{0,4},{4,8},{8,12},{12,16},{16,20},{20,24},{24,28},{28,32},{32,36}... | collective-permute-start | bytes 786440 | tf_op jit(solution)/shard_map/ppermute | solution.py:15
  49.5 3.3 collective-permute-done.1
  53.1 9.1 %while.36 = (s32[]{:T(128)}, f32[256,256]{1,0:T(8,128)S(1)}, f32[256,256]{1,0:T(8,128)S(1)}, s32[]{:T(128)}) while((s32[]{:T(128)}, f32[256,256]{1,0:T(8,128)S(1)}, f32[256,256]{1,0:T(8,128)S(1)}, s32[]{:T(128)}) %tuple.159), condition=%wide.region_3.4_spmd, body=%wide.region_2.3_spmd.sunk | while | flops 1048578 | bytes 3932213 | solution.py:31
  63.5 24.3 %all-gather.7.cloned.1.call-done = f32[1024,256]{1,0:T(8,128)} async-done(((f32[256,256]{1,0:T(8,128)}), f32[1024,256]{1,0:T(8,128)}) %all-gather.7.cloned.1.call-update) | async-done | bytes 1048592 | tf_op jit(solution)/shard_map/all_gather | solution.py:57
  91.5 4.6 %collective-permute-start.3 = (f32[256,256]{1,0:T(8,128)S(1)}, f32[256,256]{1,0:T(8,128)S(1)}, u32[]{:S(2)}, u32[]{:S(2)}) collective-permute-start(f32[256,256]{1,0:T(8,128)S(1)} %fusion.47), channel_id=1, source_target_pairs={{0,4},{4,8},{8,12},{12,16},{16,20},{20,24},{24,28},{28,32},{32,36}... | collective-permute-start | bytes 786440 | tf_op jit(solution)/shard_map/ppermute | solution.py:15
  96.8 2.6 collective-permute-done.3
  101.5 342.2 %while.37 = (s32[]{:T(128)}, f32[256,256]{1,0:T(8,128)}, f32[256,256]{1,0:T(8,128)S(1)}, pred[]{:T(512)}, f32[256,256]{1,0:T(8,128)S(1)}, /*index=5*/f32[256,256...) while((s32[]{:T(128)}, f32[256,256]{1,0:T(8,128)}, f32[256,256]{1,0:T(8,128)S(1)}, ...), condition=%wide.region_5.6_spmd.clone, body=%wide.region_4.5_spmd.clone.sunk | while | flops 1310723 | bytes 7602348 | solution.py:41
  101.6 4.4 collective-permute-start
  106.0 3.3 collective-permute-done
  110.3 4.4 collective-permute-start
  114.7 4.1 collective-permute-done
  119.8 3.5 collective-permute-start
  123.4 6.3 %collective-permute-done = f32[256,256]{1,0:T(8,128)S(1)} collective-permute-done((f32[256,256]{1,0:T(8,128)S(1)}, f32[256,256]{1,0:T(8,128)S(1)}, u32[]{:S(2)}, u32[]{:S(2)}) %collective-permute-start) | collective-permute-done | bytes 262176 | tf_op jit(solution)/shard_map/while/body/eval_jaxpr/ppermute | solution.py:15
  132.5 7.9 %collective-permute-done = f32[256,256]{1,0:T(8,128)S(1)} collective-permute-done((f32[256,256]{1,0:T(8,128)S(1)}, f32[256,256]{1,0:T(8,128)S(1)}, u32[]{:S(2)}, u32[]{:S(2)}) %collective-permute-start) | collective-permute-done | bytes 262176 | tf_op jit(solution)/shard_map/while/body/eval_jaxpr/ppermute | solution.py:15
  143.3 7.9 %collective-permute-done = f32[256,256]{1,0:T(8,128)S(1)} collective-permute-done((f32[256,256]{1,0:T(8,128)S(1)}, f32[256,256]{1,0:T(8,128)S(1)}, u32[]{:S(2)}, u32[]{:S(2)}) %collective-permute-start) | collective-permute-done | bytes 262176 | tf_op jit(solution)/shard_map/while/body/eval_jaxpr/ppermute | solution.py:15
  152.2 1.9 collective-permute-start
  154.1 7.9 %collective-permute-done = f32[256,256]{1,0:T(8,128)S(1)} collective-permute-done((f32[256,256]{1,0:T(8,128)S(1)}, f32[256,256]{1,0:T(8,128)S(1)}, u32[]{:S(2)}, u32[]{:S(2)}) %collective-permute-start) | collective-permute-done | bytes 262176 | tf_op jit(solution)/shard_map/while/body/eval_jaxpr/ppermute | solution.py:15
  164.9 7.9 %collective-permute-done = f32[256,256]{1,0:T(8,128)S(1)} collective-permute-done((f32[256,256]{1,0:T(8,128)S(1)}, f32[256,256]{1,0:T(8,128)S(1)}, u32[]{:S(2)}, u32[]{:S(2)}) %collective-permute-start) | collective-permute-done | bytes 262176 | tf_op jit(solution)/shard_map/while/body/eval_jaxpr/ppermute | solution.py:15
  175.7 7.9 %collective-permute-done = f32[256,256]{1,0:T(8,128)S(1)} collective-permute-done((f32[256,256]{1,0:T(8,128)S(1)}, f32[256,256]{1,0:T(8,128)S(1)}, u32[]{:S(2)}, u32[]{:S(2)}) %collective-permute-start) | collective-permute-done | bytes 262176 | tf_op jit(solution)/shard_map/while/body/eval_jaxpr/ppermute | solution.py:15
  184.6 1.9 collective-permute-start
  186.5 7.9 %collective-permute-done = f32[256,256]{1,0:T(8,128)S(1)} collective-permute-done((f32[256,256]{1,0:T(8,128)S(1)}, f32[256,256]{1,0:T(8,128)S(1)}, u32[]{:S(2)}, u32[]{:S(2)}) %collective-permute-start) | collective-permute-done | bytes 262176 | tf_op jit(solution)/shard_map/while/body/eval_jaxpr/ppermute | solution.py:15
  197.3 7.9 %collective-permute-done = f32[256,256]{1,0:T(8,128)S(1)} collective-permute-done((f32[256,256]{1,0:T(8,128)S(1)}, f32[256,256]{1,0:T(8,128)S(1)}, u32[]{:S(2)}, u32[]{:S(2)}) %collective-permute-start) | collective-permute-done | bytes 262176 | tf_op jit(solution)/shard_map/while/body/eval_jaxpr/ppermute | solution.py:15
  208.1 7.9 %collective-permute-done = f32[256,256]{1,0:T(8,128)S(1)} collective-permute-done((f32[256,256]{1,0:T(8,128)S(1)}, f32[256,256]{1,0:T(8,128)S(1)}, u32[]{:S(2)}, u32[]{:S(2)}) %collective-permute-start) | collective-permute-done | bytes 262176 | tf_op jit(solution)/shard_map/while/body/eval_jaxpr/ppermute | solution.py:15
  217.0 1.9 collective-permute-start
  218.9 7.9 %collective-permute-done = f32[256,256]{1,0:T(8,128)S(1)} collective-permute-done((f32[256,256]{1,0:T(8,128)S(1)}, f32[256,256]{1,0:T(8,128)S(1)}, u32[]{:S(2)}, u32[]{:S(2)}) %collective-permute-start) | collective-permute-done | bytes 262176 | tf_op jit(solution)/shard_map/while/body/eval_jaxpr/ppermute | solution.py:15
  229.7 7.9 %collective-permute-done = f32[256,256]{1,0:T(8,128)S(1)} collective-permute-done((f32[256,256]{1,0:T(8,128)S(1)}, f32[256,256]{1,0:T(8,128)S(1)}, u32[]{:S(2)}, u32[]{:S(2)}) %collective-permute-start) | collective-permute-done | bytes 262176 | tf_op jit(solution)/shard_map/while/body/eval_jaxpr/ppermute | solution.py:15
  240.5 7.9 %collective-permute-done = f32[256,256]{1,0:T(8,128)S(1)} collective-permute-done((f32[256,256]{1,0:T(8,128)S(1)}, f32[256,256]{1,0:T(8,128)S(1)}, u32[]{:S(2)}, u32[]{:S(2)}) %collective-permute-start) | collective-permute-done | bytes 262176 | tf_op jit(solution)/shard_map/while/body/eval_jaxpr/ppermute | solution.py:15
  251.3 7.9 %collective-permute-done = f32[256,256]{1,0:T(8,128)S(1)} collective-permute-done((f32[256,256]{1,0:T(8,128)S(1)}, f32[256,256]{1,0:T(8,128)S(1)}, u32[]{:S(2)}, u32[]{:S(2)}) %collective-permute-start) | collective-permute-done | bytes 262176 | tf_op jit(solution)/shard_map/while/body/eval_jaxpr/ppermute | solution.py:15
  262.1 7.9 %collective-permute-done = f32[256,256]{1,0:T(8,128)S(1)} collective-permute-done((f32[256,256]{1,0:T(8,128)S(1)}, f32[256,256]{1,0:T(8,128)S(1)}, u32[]{:S(2)}, u32[]{:S(2)}) %collective-permute-start) | collective-permute-done | bytes 262176 | tf_op jit(solution)/shard_map/while/body/eval_jaxpr/ppermute | solution.py:15
  272.9 7.9 %collective-permute-done = f32[256,256]{1,0:T(8,128)S(1)} collective-permute-done((f32[256,256]{1,0:T(8,128)S(1)}, f32[256,256]{1,0:T(8,128)S(1)}, u32[]{:S(2)}, u32[]{:S(2)}) %collective-permute-start) | collective-permute-done | bytes 262176 | tf_op jit(solution)/shard_map/while/body/eval_jaxpr/ppermute | solution.py:15
  283.8 7.9 %collective-permute-done = f32[256,256]{1,0:T(8,128)S(1)} collective-permute-done((f32[256,256]{1,0:T(8,128)S(1)}, f32[256,256]{1,0:T(8,128)S(1)}, u32[]{:S(2)}, u32[]{:S(2)}) %collective-permute-start) | collective-permute-done | bytes 262176 | tf_op jit(solution)/shard_map/while/body/eval_jaxpr/ppermute | solution.py:15
  294.6 7.9 %collective-permute-done = f32[256,256]{1,0:T(8,128)S(1)} collective-permute-done((f32[256,256]{1,0:T(8,128)S(1)}, f32[256,256]{1,0:T(8,128)S(1)}, u32[]{:S(2)}, u32[]{:S(2)}) %collective-permute-start) | collective-permute-done | bytes 262176 | tf_op jit(solution)/shard_map/while/body/eval_jaxpr/ppermute | solution.py:15
  305.4 7.9 %collective-permute-done = f32[256,256]{1,0:T(8,128)S(1)} collective-permute-done((f32[256,256]{1,0:T(8,128)S(1)}, f32[256,256]{1,0:T(8,128)S(1)}, u32[]{:S(2)}, u32[]{:S(2)}) %collective-permute-start) | collective-permute-done | bytes 262176 | tf_op jit(solution)/shard_map/while/body/eval_jaxpr/ppermute | solution.py:15
  316.2 7.9 %collective-permute-done = f32[256,256]{1,0:T(8,128)S(1)} collective-permute-done((f32[256,256]{1,0:T(8,128)S(1)}, f32[256,256]{1,0:T(8,128)S(1)}, u32[]{:S(2)}, u32[]{:S(2)}) %collective-permute-start) | collective-permute-done | bytes 262176 | tf_op jit(solution)/shard_map/while/body/eval_jaxpr/ppermute | solution.py:15
  327.0 7.9 %collective-permute-done = f32[256,256]{1,0:T(8,128)S(1)} collective-permute-done((f32[256,256]{1,0:T(8,128)S(1)}, f32[256,256]{1,0:T(8,128)S(1)}, u32[]{:S(2)}, u32[]{:S(2)}) %collective-permute-start) | collective-permute-done | bytes 262176 | tf_op jit(solution)/shard_map/while/body/eval_jaxpr/ppermute | solution.py:15
  337.8 7.9 %collective-permute-done = f32[256,256]{1,0:T(8,128)S(1)} collective-permute-done((f32[256,256]{1,0:T(8,128)S(1)}, f32[256,256]{1,0:T(8,128)S(1)}, u32[]{:S(2)}, u32[]{:S(2)}) %collective-permute-start) | collective-permute-done | bytes 262176 | tf_op jit(solution)/shard_map/while/body/eval_jaxpr/ppermute | solution.py:15
  348.6 7.9 %collective-permute-done = f32[256,256]{1,0:T(8,128)S(1)} collective-permute-done((f32[256,256]{1,0:T(8,128)S(1)}, f32[256,256]{1,0:T(8,128)S(1)}, u32[]{:S(2)}, u32[]{:S(2)}) %collective-permute-start) | collective-permute-done | bytes 262176 | tf_op jit(solution)/shard_map/while/body/eval_jaxpr/ppermute | solution.py:15
  359.4 7.9 %collective-permute-done = f32[256,256]{1,0:T(8,128)S(1)} collective-permute-done((f32[256,256]{1,0:T(8,128)S(1)}, f32[256,256]{1,0:T(8,128)S(1)}, u32[]{:S(2)}, u32[]{:S(2)}) %collective-permute-start) | collective-permute-done | bytes 262176 | tf_op jit(solution)/shard_map/while/body/eval_jaxpr/ppermute | solution.py:15
  370.2 7.9 %collective-permute-done = f32[256,256]{1,0:T(8,128)S(1)} collective-permute-done((f32[256,256]{1,0:T(8,128)S(1)}, f32[256,256]{1,0:T(8,128)S(1)}, u32[]{:S(2)}, u32[]{:S(2)}) %collective-permute-start) | collective-permute-done | bytes 262176 | tf_op jit(solution)/shard_map/while/body/eval_jaxpr/ppermute | solution.py:15
  381.0 7.9 %collective-permute-done = f32[256,256]{1,0:T(8,128)S(1)} collective-permute-done((f32[256,256]{1,0:T(8,128)S(1)}, f32[256,256]{1,0:T(8,128)S(1)}, u32[]{:S(2)}, u32[]{:S(2)}) %collective-permute-start) | collective-permute-done | bytes 262176 | tf_op jit(solution)/shard_map/while/body/eval_jaxpr/ppermute | solution.py:15
  391.8 7.9 %collective-permute-done = f32[256,256]{1,0:T(8,128)S(1)} collective-permute-done((f32[256,256]{1,0:T(8,128)S(1)}, f32[256,256]{1,0:T(8,128)S(1)}, u32[]{:S(2)}, u32[]{:S(2)}) %collective-permute-start) | collective-permute-done | bytes 262176 | tf_op jit(solution)/shard_map/while/body/eval_jaxpr/ppermute | solution.py:15
  402.6 7.9 %collective-permute-done = f32[256,256]{1,0:T(8,128)S(1)} collective-permute-done((f32[256,256]{1,0:T(8,128)S(1)}, f32[256,256]{1,0:T(8,128)S(1)}, u32[]{:S(2)}, u32[]{:S(2)}) %collective-permute-start) | collective-permute-done | bytes 262176 | tf_op jit(solution)/shard_map/while/body/eval_jaxpr/ppermute | solution.py:15
  413.4 7.9 %collective-permute-done = f32[256,256]{1,0:T(8,128)S(1)} collective-permute-done((f32[256,256]{1,0:T(8,128)S(1)}, f32[256,256]{1,0:T(8,128)S(1)}, u32[]{:S(2)}, u32[]{:S(2)}) %collective-permute-start) | collective-permute-done | bytes 262176 | tf_op jit(solution)/shard_map/while/body/eval_jaxpr/ppermute | solution.py:15
  424.2 7.9 %collective-permute-done = f32[256,256]{1,0:T(8,128)S(1)} collective-permute-done((f32[256,256]{1,0:T(8,128)S(1)}, f32[256,256]{1,0:T(8,128)S(1)}, u32[]{:S(2)}, u32[]{:S(2)}) %collective-permute-start) | collective-permute-done | bytes 262176 | tf_op jit(solution)/shard_map/while/body/eval_jaxpr/ppermute | solution.py:15
  435.0 7.9 %collective-permute-done = f32[256,256]{1,0:T(8,128)S(1)} collective-permute-done((f32[256,256]{1,0:T(8,128)S(1)}, f32[256,256]{1,0:T(8,128)S(1)}, u32[]{:S(2)}, u32[]{:S(2)}) %collective-permute-start) | collective-permute-done | bytes 262176 | tf_op jit(solution)/shard_map/while/body/eval_jaxpr/ppermute | solution.py:15
  (558 shorter events, 110.4 us)
Async XLA Ops:
  7.2 36.7 %all-gather.5.cloned.1.call-start = ((), (), s32[]{:S(2)}) async-start(), calls=%async_computation | async-start | bytes 1310720 | tf_op jit(solution)/shard_map/all_gather | solution.py:58
  7.2 1.0 copy-start.3
  17.4 0.7 copy-start.2
  18.1 34.6 %copy-start.4 = (f32[256,256]{1,0:T(8,128)S(1)}, f32[256,256]{1,0:T(8,128)}, u32[]{:S(2)}) copy-start(f32[256,256]{1,0:T(8,128)} %param.9) | copy-start | bytes 786436
  18.1 69.6 %all-gather.7.cloned.1.call-start = ((), (), s32[]{:S(2)}) async-start(), calls=%async_computation.1 | async-start | bytes 1310720 | tf_op jit(solution)/shard_map/all_gather | solution.py:57
  18.2 31.3 %collective-permute-start.2 = (f32[256,256]{1,0:T(8,128)}, f32[256,256]{1,0:T(8,128)S(1)}, u32[]{:S(2)}, u32[]{:S(2)}) collective-permute-start(f32[256,256]{1,0:T(8,128)} %copy-done.2), channel_id=1, source_target_pairs={{0,1},{1,2},{2,3},{3,4},{4,5},{5,6},{6,7},{7,8},{8,9},{9,10},{10,1... | collective-permute-start | bytes 786440 | tf_op jit(solution)/shard_map/ppermute | solution.py:15
  44.9 7.9 %collective-permute-start.1 = (f32[256,256]{1,0:T(8,128)S(1)}, f32[256,256]{1,0:T(8,128)S(1)}, u32[]{:S(2)}, u32[]{:S(2)}) collective-permute-start(f32[256,256]{1,0:T(8,128)S(1)} %slice.536), channel_id=1, source_target_pairs={{0,4},{4,8},{8,12},{12,16},{16,20},{20,24},{24,28},{28,32},{32,36}... | collective-permute-start | bytes 786440 | tf_op jit(solution)/shard_map/ppermute | solution.py:15
  89.0 1.2 copy-start.5
  91.5 5.3 %copy-start.6 = (f32[256,256]{1,0:T(8,128)}, f32[256,256]{1,0:T(8,128)S(1)}, u32[]{:S(2)}) copy-start(f32[256,256]{1,0:T(8,128)S(1)} %fusion.47) | copy-start | bytes 786436
  91.5 7.9 %collective-permute-start.3 = (f32[256,256]{1,0:T(8,128)S(1)}, f32[256,256]{1,0:T(8,128)S(1)}, u32[]{:S(2)}, u32[]{:S(2)}) collective-permute-start(f32[256,256]{1,0:T(8,128)S(1)} %fusion.47), channel_id=1, source_target_pairs={{0,4},{4,8},{8,12},{12,16},{16,20},{20,24},{24,28},{28,32},{32,36}... | collective-permute-start | bytes 786440 | tf_op jit(solution)/shard_map/ppermute | solution.py:15
  101.6 7.7 %collective-permute-start = (f32[256,256]{1,0:T(8,128)S(1)}, f32[256,256]{1,0:T(8,128)S(1)}, u32[]{:S(2)}, u32[]{:S(2)}) collective-permute-start(f32[256,256]{1,0:T(8,128)S(1)} %broadcast_select_fusion.7), channel_id=1, source_target_pairs={{0,4},{4,8},{8,12},{12,16},{16,20},{20,24},{24,28},{28,32},{32,36}... | collective-permute-start | bytes 786440 | tf_op jit(solution)/shard_map/while/body/eval_jaxpr/ppermute | solution.py:15
  110.3 8.5 %collective-permute-start = (f32[256,256]{1,0:T(8,128)S(1)}, f32[256,256]{1,0:T(8,128)S(1)}, u32[]{:S(2)}, u32[]{:S(2)}) collective-permute-start(f32[256,256]{1,0:T(8,128)S(1)} %broadcast_select_fusion.7), channel_id=1, source_target_pairs={{0,4},{4,8},{8,12},{12,16},{16,20},{20,24},{24,28},{28,32},{32,36}... | collective-permute-start | bytes 786440 | tf_op jit(solution)/shard_map/while/body/eval_jaxpr/ppermute | solution.py:15
  119.8 9.8 %collective-permute-start = (f32[256,256]{1,0:T(8,128)S(1)}, f32[256,256]{1,0:T(8,128)S(1)}, u32[]{:S(2)}, u32[]{:S(2)}) collective-permute-start(f32[256,256]{1,0:T(8,128)S(1)} %broadcast_select_fusion.7), channel_id=1, source_target_pairs={{0,4},{4,8},{8,12},{12,16},{16,20},{20,24},{24,28},{28,32},{32,36}... | collective-permute-start | bytes 786440 | tf_op jit(solution)/shard_map/while/body/eval_jaxpr/ppermute | solution.py:15
  130.6 9.8 %collective-permute-start = (f32[256,256]{1,0:T(8,128)S(1)}, f32[256,256]{1,0:T(8,128)S(1)}, u32[]{:S(2)}, u32[]{:S(2)}) collective-permute-start(f32[256,256]{1,0:T(8,128)S(1)} %broadcast_select_fusion.7), channel_id=1, source_target_pairs={{0,4},{4,8},{8,12},{12,16},{16,20},{20,24},{24,28},{28,32},{32,36}... | collective-permute-start | bytes 786440 | tf_op jit(solution)/shard_map/while/body/eval_jaxpr/ppermute | solution.py:15
  140.5 0.7 copy-start
  141.4 9.8 %collective-permute-start = (f32[256,256]{1,0:T(8,128)S(1)}, f32[256,256]{1,0:T(8,128)S(1)}, u32[]{:S(2)}, u32[]{:S(2)}) collective-permute-start(f32[256,256]{1,0:T(8,128)S(1)} %broadcast_select_fusion.7), channel_id=1, source_target_pairs={{0,4},{4,8},{8,12},{12,16},{16,20},{20,24},{24,28},{28,32},{32,36}... | collective-permute-start | bytes 786440 | tf_op jit(solution)/shard_map/while/body/eval_jaxpr/ppermute | solution.py:15
  152.2 9.8 %collective-permute-start = (f32[256,256]{1,0:T(8,128)S(1)}, f32[256,256]{1,0:T(8,128)S(1)}, u32[]{:S(2)}, u32[]{:S(2)}) collective-permute-start(f32[256,256]{1,0:T(8,128)S(1)} %broadcast_select_fusion.7), channel_id=1, source_target_pairs={{0,4},{4,8},{8,12},{12,16},{16,20},{20,24},{24,28},{28,32},{32,36}... | collective-permute-start | bytes 786440 | tf_op jit(solution)/shard_map/while/body/eval_jaxpr/ppermute | solution.py:15
  163.0 9.8 %collective-permute-start = (f32[256,256]{1,0:T(8,128)S(1)}, f32[256,256]{1,0:T(8,128)S(1)}, u32[]{:S(2)}, u32[]{:S(2)}) collective-permute-start(f32[256,256]{1,0:T(8,128)S(1)} %broadcast_select_fusion.7), channel_id=1, source_target_pairs={{0,4},{4,8},{8,12},{12,16},{16,20},{20,24},{24,28},{28,32},{32,36}... | collective-permute-start | bytes 786440 | tf_op jit(solution)/shard_map/while/body/eval_jaxpr/ppermute | solution.py:15
  172.9 0.7 copy-start
  173.8 9.8 %collective-permute-start = (f32[256,256]{1,0:T(8,128)S(1)}, f32[256,256]{1,0:T(8,128)S(1)}, u32[]{:S(2)}, u32[]{:S(2)}) collective-permute-start(f32[256,256]{1,0:T(8,128)S(1)} %broadcast_select_fusion.7), channel_id=1, source_target_pairs={{0,4},{4,8},{8,12},{12,16},{16,20},{20,24},{24,28},{28,32},{32,36}... | collective-permute-start | bytes 786440 | tf_op jit(solution)/shard_map/while/body/eval_jaxpr/ppermute | solution.py:15
  184.6 9.8 %collective-permute-start = (f32[256,256]{1,0:T(8,128)S(1)}, f32[256,256]{1,0:T(8,128)S(1)}, u32[]{:S(2)}, u32[]{:S(2)}) collective-permute-start(f32[256,256]{1,0:T(8,128)S(1)} %broadcast_select_fusion.7), channel_id=1, source_target_pairs={{0,4},{4,8},{8,12},{12,16},{16,20},{20,24},{24,28},{28,32},{32,36}... | collective-permute-start | bytes 786440 | tf_op jit(solution)/shard_map/while/body/eval_jaxpr/ppermute | solution.py:15
  195.4 9.8 %collective-permute-start = (f32[256,256]{1,0:T(8,128)S(1)}, f32[256,256]{1,0:T(8,128)S(1)}, u32[]{:S(2)}, u32[]{:S(2)}) collective-permute-start(f32[256,256]{1,0:T(8,128)S(1)} %broadcast_select_fusion.7), channel_id=1, source_target_pairs={{0,4},{4,8},{8,12},{12,16},{16,20},{20,24},{24,28},{28,32},{32,36}... | collective-permute-start | bytes 786440 | tf_op jit(solution)/shard_map/while/body/eval_jaxpr/ppermute | solution.py:15
  206.2 9.8 %collective-permute-start = (f32[256,256]{1,0:T(8,128)S(1)}, f32[256,256]{1,0:T(8,128)S(1)}, u32[]{:S(2)}, u32[]{:S(2)}) collective-permute-start(f32[256,256]{1,0:T(8,128)S(1)} %broadcast_select_fusion.7), channel_id=1, source_target_pairs={{0,4},{4,8},{8,12},{12,16},{16,20},{20,24},{24,28},{28,32},{32,36}... | collective-permute-start | bytes 786440 | tf_op jit(solution)/shard_map/while/body/eval_jaxpr/ppermute | solution.py:15
  217.0 9.8 %collective-permute-start = (f32[256,256]{1,0:T(8,128)S(1)}, f32[256,256]{1,0:T(8,128)S(1)}, u32[]{:S(2)}, u32[]{:S(2)}) collective-permute-start(f32[256,256]{1,0:T(8,128)S(1)} %broadcast_select_fusion.7), channel_id=1, source_target_pairs={{0,4},{4,8},{8,12},{12,16},{16,20},{20,24},{24,28},{28,32},{32,36}... | collective-permute-start | bytes 786440 | tf_op jit(solution)/shard_map/while/body/eval_jaxpr/ppermute | solution.py:15
  227.8 9.8 %collective-permute-start = (f32[256,256]{1,0:T(8,128)S(1)}, f32[256,256]{1,0:T(8,128)S(1)}, u32[]{:S(2)}, u32[]{:S(2)}) collective-permute-start(f32[256,256]{1,0:T(8,128)S(1)} %broadcast_select_fusion.7), channel_id=1, source_target_pairs={{0,4},{4,8},{8,12},{12,16},{16,20},{20,24},{24,28},{28,32},{32,36}... | collective-permute-start | bytes 786440 | tf_op jit(solution)/shard_map/while/body/eval_jaxpr/ppermute | solution.py:15
  238.6 9.8 %collective-permute-start = (f32[256,256]{1,0:T(8,128)S(1)}, f32[256,256]{1,0:T(8,128)S(1)}, u32[]{:S(2)}, u32[]{:S(2)}) collective-permute-start(f32[256,256]{1,0:T(8,128)S(1)} %broadcast_select_fusion.7), channel_id=1, source_target_pairs={{0,4},{4,8},{8,12},{12,16},{16,20},{20,24},{24,28},{28,32},{32,36}... | collective-permute-start | bytes 786440 | tf_op jit(solution)/shard_map/while/body/eval_jaxpr/ppermute | solution.py:15
  249.4 9.8 %collective-permute-start = (f32[256,256]{1,0:T(8,128)S(1)}, f32[256,256]{1,0:T(8,128)S(1)}, u32[]{:S(2)}, u32[]{:S(2)}) collective-permute-start(f32[256,256]{1,0:T(8,128)S(1)} %broadcast_select_fusion.7), channel_id=1, source_target_pairs={{0,4},{4,8},{8,12},{12,16},{16,20},{20,24},{24,28},{28,32},{32,36}... | collective-permute-start | bytes 786440 | tf_op jit(solution)/shard_map/while/body/eval_jaxpr/ppermute | solution.py:15
  260.2 9.8 %collective-permute-start = (f32[256,256]{1,0:T(8,128)S(1)}, f32[256,256]{1,0:T(8,128)S(1)}, u32[]{:S(2)}, u32[]{:S(2)}) collective-permute-start(f32[256,256]{1,0:T(8,128)S(1)} %broadcast_select_fusion.7), channel_id=1, source_target_pairs={{0,4},{4,8},{8,12},{12,16},{16,20},{20,24},{24,28},{28,32},{32,36}... | collective-permute-start | bytes 786440 | tf_op jit(solution)/shard_map/while/body/eval_jaxpr/ppermute | solution.py:15
  271.0 9.8 %collective-permute-start = (f32[256,256]{1,0:T(8,128)S(1)}, f32[256,256]{1,0:T(8,128)S(1)}, u32[]{:S(2)}, u32[]{:S(2)}) collective-permute-start(f32[256,256]{1,0:T(8,128)S(1)} %broadcast_select_fusion.7), channel_id=1, source_target_pairs={{0,4},{4,8},{8,12},{12,16},{16,20},{20,24},{24,28},{28,32},{32,36}... | collective-permute-start | bytes 786440 | tf_op jit(solution)/shard_map/while/body/eval_jaxpr/ppermute | solution.py:15
  281.8 9.8 %collective-permute-start = (f32[256,256]{1,0:T(8,128)S(1)}, f32[256,256]{1,0:T(8,128)S(1)}, u32[]{:S(2)}, u32[]{:S(2)}) collective-permute-start(f32[256,256]{1,0:T(8,128)S(1)} %broadcast_select_fusion.7), channel_id=1, source_target_pairs={{0,4},{4,8},{8,12},{12,16},{16,20},{20,24},{24,28},{28,32},{32,36}... | collective-permute-start | bytes 786440 | tf_op jit(solution)/shard_map/while/body/eval_jaxpr/ppermute | solution.py:15
  292.6 9.8 %collective-permute-start = (f32[256,256]{1,0:T(8,128)S(1)}, f32[256,256]{1,0:T(8,128)S(1)}, u32[]{:S(2)}, u32[]{:S(2)}) collective-permute-start(f32[256,256]{1,0:T(8,128)S(1)} %broadcast_select_fusion.7), channel_id=1, source_target_pairs={{0,4},{4,8},{8,12},{12,16},{16,20},{20,24},{24,28},{28,32},{32,36}... | collective-permute-start | bytes 786440 | tf_op jit(solution)/shard_map/while/body/eval_jaxpr/ppermute | solution.py:15
  303.4 9.8 %collective-permute-start = (f32[256,256]{1,0:T(8,128)S(1)}, f32[256,256]{1,0:T(8,128)S(1)}, u32[]{:S(2)}, u32[]{:S(2)}) collective-permute-start(f32[256,256]{1,0:T(8,128)S(1)} %broadcast_select_fusion.7), channel_id=1, source_target_pairs={{0,4},{4,8},{8,12},{12,16},{16,20},{20,24},{24,28},{28,32},{32,36}... | collective-permute-start | bytes 786440 | tf_op jit(solution)/shard_map/while/body/eval_jaxpr/ppermute | solution.py:15
  313.3 0.7 copy-start
  314.2 9.8 %collective-permute-start = (f32[256,256]{1,0:T(8,128)S(1)}, f32[256,256]{1,0:T(8,128)S(1)}, u32[]{:S(2)}, u32[]{:S(2)}) collective-permute-start(f32[256,256]{1,0:T(8,128)S(1)} %broadcast_select_fusion.7), channel_id=1, source_target_pairs={{0,4},{4,8},{8,12},{12,16},{16,20},{20,24},{24,28},{28,32},{32,36}... | collective-permute-start | bytes 786440 | tf_op jit(solution)/shard_map/while/body/eval_jaxpr/ppermute | solution.py:15
  325.0 9.8 %collective-permute-start = (f32[256,256]{1,0:T(8,128)S(1)}, f32[256,256]{1,0:T(8,128)S(1)}, u32[]{:S(2)}, u32[]{:S(2)}) collective-permute-start(f32[256,256]{1,0:T(8,128)S(1)} %broadcast_select_fusion.7), channel_id=1, source_target_pairs={{0,4},{4,8},{8,12},{12,16},{16,20},{20,24},{24,28},{28,32},{32,36}... | collective-permute-start | bytes 786440 | tf_op jit(solution)/shard_map/while/body/eval_jaxpr/ppermute | solution.py:15
  335.8 9.8 %collective-permute-start = (f32[256,256]{1,0:T(8,128)S(1)}, f32[256,256]{1,0:T(8,128)S(1)}, u32[]{:S(2)}, u32[]{:S(2)}) collective-permute-start(f32[256,256]{1,0:T(8,128)S(1)} %broadcast_select_fusion.7), channel_id=1, source_target_pairs={{0,4},{4,8},{8,12},{12,16},{16,20},{20,24},{24,28},{28,32},{32,36}... | collective-permute-start | bytes 786440 | tf_op jit(solution)/shard_map/while/body/eval_jaxpr/ppermute | solution.py:15
  345.7 0.7 copy-start
  346.6 9.8 %collective-permute-start = (f32[256,256]{1,0:T(8,128)S(1)}, f32[256,256]{1,0:T(8,128)S(1)}, u32[]{:S(2)}, u32[]{:S(2)}) collective-permute-start(f32[256,256]{1,0:T(8,128)S(1)} %broadcast_select_fusion.7), channel_id=1, source_target_pairs={{0,4},{4,8},{8,12},{12,16},{16,20},{20,24},{24,28},{28,32},{32,36}... | collective-permute-start | bytes 786440 | tf_op jit(solution)/shard_map/while/body/eval_jaxpr/ppermute | solution.py:15
  357.4 9.8 %collective-permute-start = (f32[256,256]{1,0:T(8,128)S(1)}, f32[256,256]{1,0:T(8,128)S(1)}, u32[]{:S(2)}, u32[]{:S(2)}) collective-permute-start(f32[256,256]{1,0:T(8,128)S(1)} %broadcast_select_fusion.7), channel_id=1, source_target_pairs={{0,4},{4,8},{8,12},{12,16},{16,20},{20,24},{24,28},{28,32},{32,36}... | collective-permute-start | bytes 786440 | tf_op jit(solution)/shard_map/while/body/eval_jaxpr/ppermute | solution.py:15
  368.2 9.8 %collective-permute-start = (f32[256,256]{1,0:T(8,128)S(1)}, f32[256,256]{1,0:T(8,128)S(1)}, u32[]{:S(2)}, u32[]{:S(2)}) collective-permute-start(f32[256,256]{1,0:T(8,128)S(1)} %broadcast_select_fusion.7), channel_id=1, source_target_pairs={{0,4},{4,8},{8,12},{12,16},{16,20},{20,24},{24,28},{28,32},{32,36}... | collective-permute-start | bytes 786440 | tf_op jit(solution)/shard_map/while/body/eval_jaxpr/ppermute | solution.py:15
  378.1 0.7 copy-start
  379.0 9.8 %collective-permute-start = (f32[256,256]{1,0:T(8,128)S(1)}, f32[256,256]{1,0:T(8,128)S(1)}, u32[]{:S(2)}, u32[]{:S(2)}) collective-permute-start(f32[256,256]{1,0:T(8,128)S(1)} %broadcast_select_fusion.7), channel_id=1, source_target_pairs={{0,4},{4,8},{8,12},{12,16},{16,20},{20,24},{24,28},{28,32},{32,36}... | collective-permute-start | bytes 786440 | tf_op jit(solution)/shard_map/while/body/eval_jaxpr/ppermute | solution.py:15
  389.8 9.8 %collective-permute-start = (f32[256,256]{1,0:T(8,128)S(1)}, f32[256,256]{1,0:T(8,128)S(1)}, u32[]{:S(2)}, u32[]{:S(2)}) collective-permute-start(f32[256,256]{1,0:T(8,128)S(1)} %broadcast_select_fusion.7), channel_id=1, source_target_pairs={{0,4},{4,8},{8,12},{12,16},{16,20},{20,24},{24,28},{28,32},{32,36}... | collective-permute-start | bytes 786440 | tf_op jit(solution)/shard_map/while/body/eval_jaxpr/ppermute | solution.py:15
  400.6 9.8 %collective-permute-start = (f32[256,256]{1,0:T(8,128)S(1)}, f32[256,256]{1,0:T(8,128)S(1)}, u32[]{:S(2)}, u32[]{:S(2)}) collective-permute-start(f32[256,256]{1,0:T(8,128)S(1)} %broadcast_select_fusion.7), channel_id=1, source_target_pairs={{0,4},{4,8},{8,12},{12,16},{16,20},{20,24},{24,28},{28,32},{32,36}... | collective-permute-start | bytes 786440 | tf_op jit(solution)/shard_map/while/body/eval_jaxpr/ppermute | solution.py:15
  411.4 9.8 %collective-permute-start = (f32[256,256]{1,0:T(8,128)S(1)}, f32[256,256]{1,0:T(8,128)S(1)}, u32[]{:S(2)}, u32[]{:S(2)}) collective-permute-start(f32[256,256]{1,0:T(8,128)S(1)} %broadcast_select_fusion.7), channel_id=1, source_target_pairs={{0,4},{4,8},{8,12},{12,16},{16,20},{20,24},{24,28},{28,32},{32,36}... | collective-permute-start | bytes 786440 | tf_op jit(solution)/shard_map/while/body/eval_jaxpr/ppermute | solution.py:15
  422.2 9.8 %collective-permute-start = (f32[256,256]{1,0:T(8,128)S(1)}, f32[256,256]{1,0:T(8,128)S(1)}, u32[]{:S(2)}, u32[]{:S(2)}) collective-permute-start(f32[256,256]{1,0:T(8,128)S(1)} %broadcast_select_fusion.7), channel_id=1, source_target_pairs={{0,4},{4,8},{8,12},{12,16},{16,20},{20,24},{24,28},{28,32},{32,36}... | collective-permute-start | bytes 786440 | tf_op jit(solution)/shard_map/while/body/eval_jaxpr/ppermute | solution.py:15
  433.0 9.8 %collective-permute-start = (f32[256,256]{1,0:T(8,128)S(1)}, f32[256,256]{1,0:T(8,128)S(1)}, u32[]{:S(2)}, u32[]{:S(2)}) collective-permute-start(f32[256,256]{1,0:T(8,128)S(1)} %broadcast_select_fusion.7), channel_id=1, source_target_pairs={{0,4},{4,8},{8,12},{12,16},{16,20},{20,24},{24,28},{28,32},{32,36}... | collective-permute-start | bytes 786440 | tf_op jit(solution)/shard_map/while/body/eval_jaxpr/ppermute | solution.py:15
  443.8 1.2 copy-start.1
  (27 other events, 19.0 us)
Sparse Core Ops, SparseCore 0:
  18.3 25.6 all-gather.4
  63.3 24.3 all-gather.6
where the time goes:
time: 461 us; the launch traced here: 454 us
  waiting for transfers between devices  294 us (64%)
  starting transfers between devices  80.9 us (18%)
  local copies, waits for them, and re-layouts  37.5 us (8%)
  other arithmetic  22.8 us (5%)
  between operations  14.6 us (3%)
    ppermute x35, waiting for transfers between devices, passed_along(): return lax.ppermute(block, axis, route)  248 us
    ppermute x35, starting transfers between devices, passed_along(): return lax.ppermute(block, axis, route)  80.9 us
    all_gather x1, waiting for transfers between devices, local(): lax.all_gather(term[None], 'grp', axis=0, tiled=True)  24.3 us
    all_gather x1, waiting for transfers between devices, local(): lax.all_gather(relaxed[None], 'grp', axis=0, tiled=True)  22 us
    slice x150, local copies, waits for them, and re-layouts, advance(): jnp.roll(values, -1, -1)  17.8 us
    while x64, local copies, waits for them, and re-layouts  12.9 us
  transfers between devices with their start and end apart: 37, of which 36 were waited for; matrix products, arithmetic and copies ran while one was open for 0% of the time, Pallas kernels for 0%

commit v1 on v0

v1 whole, which is shorter than its diff:
```python
import functools

import jax
import jax.numpy as jnp
from jax import lax
from jax.experimental import pallas as pl
from jax.experimental.pallas import tpu as pltpu
from jax.sharding import PartitionSpec as P

STEPS = 16
KAPPA = 0.0035
MESH = pl.DeviceIdType.MESH

N = 256
LANES = 128
HALO = 40
CORE = 64
ROWS = CORE + 2 * HALO
M = ROWS // 8
MF = N // 8
STAGE = 16
F32 = jnp.float32


def at_xy(x, y, c):
    return (x * 4 + y) * 2 + c


def permutation(transposed):
    big = lax.broadcasted_iota(jnp.int32, (N, N), 1 if transposed else 0)
    new = lax.broadcasted_iota(jnp.int32, (N, N), 0 if transposed else 1)
    wanted = 2 * (new % LANES) + new // LANES
    return (big == wanted).astype(F32).astype(jnp.bfloat16)


def permuted(values, matrix):
    high = values.astype(jnp.bfloat16)
    rest = values - high.astype(F32)
    middle = rest.astype(jnp.bfloat16)
    low = (rest - middle.astype(F32)).astype(jnp.bfloat16)
    dot = functools.partial(jnp.dot, preferred_element_type=F32)
    return (dot(high, matrix) + dot(middle, matrix)) + dot(low, matrix)


def advance(state, a_ref, b_ref, scale):
    left, right = state
    m = len(left)
    new_left, new_right = [], []
    for k in range(m):
        u, v = left[k], right[k]
        above = [
            pltpu.roll(half[m - 1], 1, 0) if k == 0 else half[k - 1] for half in state
        ]
        below = [
            pltpu.roll(half[0], 7, 0) if k == m - 1 else half[k + 1] for half in state
        ]
        su = above[0] + below[0] + (v + pltpu.roll(v, 1, 1))
        sv = above[1] + below[1] + (u + pltpu.roll(u, LANES - 1, 1))
        new_left.append(scale * su + u * (a_ref[0, k] - b_ref[0, k] * (u * u)))
        new_right.append(scale * sv + v * (a_ref[1, k] - b_ref[1, k] * (v * v)))
    return new_left, new_right


def load_rows(ref, m):
    return [[ref[h, pl.ds(k, 8, stride=m), :] for k in range(m)] for h in range(2)]


def store_rows(ref, state, first=0):
    m = len(state[0])
    for h in range(2):
        for k in range(m):
            ref[h, pl.ds(first + k, 8, stride=m), :] = state[h][k]


def load_state(ref):
    return [[ref[h, k] for k in range(ref.shape[1])] for h in range(2)]


def store_state(ref, state):
    for h in range(2):
        for k in range(len(state[h])):
            ref[h, k] = state[h][k]


def plus(state, addend):
    return [[x + y for x, y in zip(s, t)] for s, t in zip(state, addend)]


def minus(state, addend):
    return [[x - y for x, y in zip(s, t)] for s, t in zip(state, addend)]


def repeat(state, a_ref, b_ref, scale, count, unroll):
    def turn(_, carried):
        carried = [list(half) for half in carried]
        for _ in range(unroll):
            carried = advance(carried, a_ref, b_ref, scale)
        return tuple(tuple(half) for half in carried)

    state = tuple(tuple(half) for half in state)
    state = lax.fori_loop(0, count // unroll, turn, state)
    return [list(half) for half in state]


def widen(ext, values):
    for h in range(2):
        part = values[:, h * LANES : (h + 1) * LANES]
        ext[h, HALO : HALO + N] = part
        ext[h, 0:HALO] = part[N - HALO :]
        ext[h, HALO + N :] = part[:HALO]


def copy_strip(dst, ext, first):
    for h in range(2):
        for row in range(0, ROWS, 8):
            src = pl.ds(pl.multiple_of(first + row, 8), 8)
            dst[h, row : row + 8] = ext[h, src]


def kernel(
    init_ref,
    rate_ref,
    guess_ref,
    points_ref,
    corner_ref,
    perm,
    init_ext,
    rate_ext,
    relaxed_ext,
    strip,
    a_full,
    b_full,
    a_1,
    b_1,
    a_16,
    b_16,
    a_64,
    b_64,
    starts,
    terms,
    corner_rows,
    corner_full,
    fresh,
    ct_rows,
    ct,
    cts,
    history,
    hop_rows,
    z_stage,
    pass_rows,
    z_in,
    z_own,
    point_rows,
    points_full,
    start_send,
    start_recv,
    corner_send,
    corner_recv,
    fresh_send,
    fresh_recv,
    ct_send,
    ct_recv,
    hop_send,
    hop_recv,
    pass_send,
    pass_recv,
    point_send,
    point_recv,
):
    group = lax.axis_index("tm")
    member = lax.axis_index("grp")
    groups = 32
    x, y, c = group // 8, (group // 2) % 4, group % 2
    stage = x // 2
    chip_x = x % 2
    local_group = group % STAGE
    core0 = c == 0

    def around(distance):
        return (member + distance) % 4

    barrier = pltpu.get_barrier_semaphore()

    def greet(tm, grp):
        pl.semaphore_signal(barrier, inc=1, device_id=(tm, grp), device_id_type=MESH)

    for d in (1, 2, 3):
        greet(group, around(d))

    @pl.when(group > 0)
    def _():
        greet(group - 1, 3)
        greet(group - 1, member)

    @pl.when(core0)
    def _():
        for dx in range(2):
            for dy in range(4):
                px, py = stage * 2 + (chip_x + dx) % 2, (y + dy) % 4
                if (dx, dy) != (0, 0):
                    greet(at_xy(px, py, 0), member)
                greet(at_xy(px, py, 1), member)

    @pl.when(jnp.logical_and(core0, stage == 1))
    def _():
        for d in (0, 1, 3):
            greet(at_xy(3 - x, y, 0), around(d))

    @pl.when(c == 1)
    def _():
        greet(group - 1, member)

    more = (group < groups - 1).astype(jnp.int32)
    expected = (
        3
        + more * (1 + 4 * (member == 3).astype(jnp.int32))
        + 7
        + c
        + (1 - c) * (1 + 3 * (1 - stage))
    )

    perm[...] = permutation(False)
    rate = permuted(rate_ref[...], perm[...])
    widen(rate_ext, rate)
    first = jnp.logical_and(group == 0, member == 0)
    prior = jnp.where(first, init_ref[...], guess_ref[0])
    widen(relaxed_ext, permuted(prior, perm[...]))
    full = relaxed_ext.at[:, HALO : HALO + N]
    rates = load_rows(rate_ext.at[:, HALO : HALO + N], MF)
    for h in range(2):
        for k in range(MF):
            a_full[h, k] = (1.0 - 4.0 * KAPPA) + rates[h][k]
            b_full[h, k] = rates[h][k]
    relaxed = repeat(load_rows(full, MF), a_full, b_full, KAPPA, STEPS, 4)
    store_rows(relaxed_ext, relaxed, HALO)
    for h in range(2):
        relaxed_ext[h, 0:HALO] = relaxed_ext[h, N : N + HALO]
        relaxed_ext[h, HALO + N :] = relaxed_ext[h, HALO : 2 * HALO]

    pl.semaphore_wait(barrier, expected)

    pending = []
    slot = (member + 1) % 4
    target = group + (member == 3).astype(jnp.int32)
    have = jnp.logical_or(member < 3, group < groups - 1)
    for d in (1, 3, 2, 0):
        q = around(d)
        copy = pltpu.make_async_remote_copy(
            src_ref=relaxed_ext.at[:, pl.ds(pl.multiple_of(q * CORE, 8), ROWS)],
            dst_ref=starts.at[slot],
            send_sem=start_send.at[d],
            recv_sem=start_recv.at[slot],
            device_id=(target, q),
            device_id_type=MESH,
        )
        when = have if d else jnp.logical_and(have, member == 3)
        pl.when(when)(copy.start)
        pending.append((when, copy))

    own_first = pl.multiple_of(member * CORE, 8)

    @pl.when(member < 3)
    def _():
        copy_strip(starts.at[slot], relaxed_ext, own_first)

    widen(init_ext, permuted(init_ref[...], perm[...]))

    @pl.when(group == 0)
    def _():
        copy_strip(starts.at[0], init_ext, own_first)
        copy_strip(fresh, init_ext, own_first)

    copy_strip(strip, rate_ext, own_first)
    rates = load_rows(strip, M)
    for h in range(2):
        for k in range(M):
            r = rates[h][k]
            for factor, a_ref, b_ref in (
                (1.0, a_1, b_1),
                (16.0, a_16, b_16),
                (64.0, a_64, b_64),
            ):
                a_ref[h, k] = (1.0 - 4.0 * KAPPA * factor) + factor * r
                b_ref[h, k] = factor * r
    copy_strip(strip, init_ext, own_first)
    perm[...] = permutation(True)

    def one_term(turn, _):
        offset = turn + (turn == 2).astype(jnp.int32) - (turn == 3).astype(jnp.int32)
        s = (member + 1 + offset) % 4
        remote = jnp.where(s == 0, group > 0, s != member + 1)

        @pl.when(remote)
        def _():
            pltpu.make_async_remote_copy(
                src_ref=starts.at[s],
                dst_ref=starts.at[s],
                send_sem=start_send.at[0],
                recv_sem=start_recv.at[s],
                device_id=(group, around(1)),
                device_id_type=MESH,
            ).wait_recv()

        start = load_rows(starts.at[s], M)
        store_state(terms.at[s], advance(start, a_16, b_16, 16.0 * KAPPA))
        fine = repeat(load_rows(starts.at[s], M), a_1, b_1, KAPPA, STEPS, 4)
        store_state(terms.at[s], minus(fine, load_state(terms.at[s])))
        return 0

    lax.fori_loop(0, 4, one_term, 0)

    def big_step(state, index):
        stepped = advance(state, a_16, b_16, 16.0 * KAPPA)
        return plus(stepped, load_state(terms.at[index]))

    corner = load_rows(starts.at[0], M)
    for index in range(4):
        corner = big_step(corner, index)
    store_rows(corner_rows, corner)
    sent = slice(HALO - 24, HALO + CORE + 24)
    copy = pltpu.make_async_remote_copy(
        src_ref=corner_rows.at[:, sent],
        dst_ref=fresh.at[:, sent],
        send_sem=fresh_send,
        recv_sem=fresh_recv,
        device_id=(lax.rem(group + 1, groups), member),
        device_id_type=MESH,
    )
    fresh_copy = copy
    pl.when(group < groups - 1)(copy.start)
    pending.append((group < groups - 1, copy))
    core_rows = slice(HALO, HALO + CORE)
    own_rows = pl.ds(own_first, CORE)
    for d in (1, 3, 2):
        copy = pltpu.make_async_remote_copy(
            src_ref=corner_rows.at[:, core_rows],
            dst_ref=corner_full.at[:, own_rows],
            send_sem=corner_send.at[d - 1],
            recv_sem=corner_recv.at[member],
            device_id=(group, around(d)),
            device_id_type=MESH,
        )
        copy.start()
        pending.append((None, copy))
    for h in range(2):
        corner_full[h, own_rows] = corner_rows[h, core_rows]

    pl.when(group > 0)(fresh_copy.wait_recv)
    state = load_rows(fresh, M)
    for index in range(4):
        state = big_step(state, index)
    state = minus(state, advance(load_rows(fresh, M), a_64, b_64, 64.0 * KAPPA))
    store_state(ct, state)
    store_rows(ct_rows, state)
    for dx in (1, 0):
        for dy in (2, 1, 3, 0):
            px, py = stage * 2 + (chip_x + dx) % 2, (y + dy) % 4
            copy = pltpu.make_async_remote_copy(
                src_ref=ct_rows.at[:, sent],
                dst_ref=cts.at[local_group, :, sent],
                send_sem=ct_send.at[dx * 4 + dy],
                recv_sem=ct_recv.at[local_group],
                device_id=(at_xy(px, py, 0), member),
                device_id_type=MESH,
            )
            when = None if (dx, dy) != (0, 0) else c == 1
            if when is None:
                copy.start()
            else:
                pl.when(when)(copy.start)
            pending.append((when, copy))

    for d in (1, 3, 2):
        q = around(d)
        pltpu.make_async_remote_copy(
            src_ref=corner_rows.at[:, core_rows],
            dst_ref=corner_full.at[:, pl.ds(pl.multiple_of(q * CORE, 8), CORE)],
            send_sem=corner_send.at[0],
            recv_sem=corner_recv.at[q],
            device_id=(group, q),
            device_id_type=MESH,
        ).wait_recv()
    both = jnp.concatenate([corner_full[0], corner_full[1]], axis=1)
    corner_ref[0] = permuted(both, perm[...])

    hop = []
    rows = 24
    for d, src, dst in (
        (3, HALO, HALO + CORE),
        (1, HALO + CORE - rows, HALO - rows),
        (0, HALO, HALO),
    ):
        count = rows if d else CORE
        hop.append(
            pltpu.make_async_remote_copy(
                src_ref=hop_rows.at[:, src : src + count],
                dst_ref=z_stage.at[:, dst : dst + count],
                send_sem=hop_send.at[d],
                recv_sem=hop_recv.at[d],
                device_id=(at_xy(3 - x, y, 0), around(d)),
                device_id_type=MESH,
            )
        )
    handed = slice(HALO - 8, HALO + CORE + 8)
    pass_copy = pltpu.make_async_remote_copy(
        src_ref=pass_rows.at[:, handed],
        dst_ref=z_in.at[:, handed],
        send_sem=pass_send,
        recv_sem=pass_recv,
        device_id=(at_xy(x, y, 1), member),
        device_id_type=MESH,
    )

    @pl.when(core0)
    def _():
        store_rows(cts.at[local_group], load_state(ct))

        @pl.when(stage == 0)
        def _():
            store_state(history.at[0], load_rows(strip, M))

        @pl.when(stage == 1)
        def _():
            for copy in hop:
                copy.wait_recv()
            store_state(history.at[0], load_rows(z_stage, M))

        def one_group(t, state):
            @pl.when(t != local_group)
            def _():
                pltpu.make_async_remote_copy(
                    src_ref=ct_rows.at[:, sent],
                    dst_ref=cts.at[t, :, sent],
                    send_sem=ct_send.at[0],
                    recv_sem=ct_recv.at[t],
                    device_id=(group, around(1)),
                    device_id_type=MESH,
                ).wait_recv()

            state = [list(half) for half in state]
            state = advance(state, a_64, b_64, 64.0 * KAPPA)
            state = plus(state, load_rows(cts.at[t], M))
            store_state(history.at[t + 1], state)
            return tuple(tuple(half) for half in state)

        begin = tuple(tuple(half) for half in load_state(history.at[0]))
        last = lax.fori_loop(0, STAGE, one_group, begin)

        @pl.when(stage == 0)
        def _():
            store_rows(hop_rows, last)
            for copy in hop:
                copy.start()

        store_rows(pass_rows, load_state(history.at[local_group + 1]))
        pass_copy.start()
        store_state(z_own, load_state(history.at[local_group]))

    @pl.when(c == 1)
    def _():
        pass_copy.wait_recv()
        store_state(z_own, load_rows(z_in, M))

    final = load_state(z_own)
    final = plus(advance(final, a_64, b_64, 64.0 * KAPPA), load_state(ct))
    state = load_state(z_own)
    for index in range(4):
        state = big_step(state, index) if index < 3 else final
        store_rows(point_rows.at[index], state)

        copy = pltpu.make_async_remote_copy(
            src_ref=point_rows.at[index, :, core_rows],
            dst_ref=points_full.at[:, own_rows],
            send_sem=point_send.at[index],
            recv_sem=point_recv.at[member],
            device_id=(group, index),
            device_id_type=MESH,
        )
        when = member != index
        pl.when(when)(copy.start)
        pending.append((when, copy))
    for h in range(2):
        points_full[h, own_rows] = point_rows[member, h, core_rows]
    for d in (1, 3, 2):
        q = around(d)
        pltpu.make_async_remote_copy(
            src_ref=point_rows.at[0, :, core_rows],
            dst_ref=points_full.at[:, pl.ds(pl.multiple_of(q * CORE, 8), CORE)],
            send_sem=point_send.at[0],
            recv_sem=point_recv.at[q],
            device_id=(group, q),
            device_id_type=MESH,
        ).wait_recv()
    both = jnp.concatenate([points_full[0], points_full[1]], axis=1)
    points_ref[0] = permuted(both, perm[...])

    for when, copy in pending:
        if when is None:
            copy.wait_send()
        else:
            pl.when(when)(copy.wait_send)

    @pl.when(core0)
    def _():
        pass_copy.wait_send()

        @pl.when(stage == 0)
        def _():
            for copy in hop:
                copy.wait_send()


def local(init_field, reaction, guesses):
    vmem = pl.BlockSpec(memory_space=pltpu.VMEM)
    strip_state = pltpu.VMEM((2, M, 8, LANES), F32)
    full_state = pltpu.VMEM((2, MF, 8, LANES), F32)
    strip_rows = pltpu.VMEM((2, ROWS, LANES), F32)
    ext_rows = pltpu.VMEM((2, N + 2 * HALO, LANES), F32)
    full_rows = pltpu.VMEM((2, N, LANES), F32)
    dma = pltpu.SemaphoreType.DMA

    def many(count, *shape):
        return pltpu.VMEM((count, *shape), F32)

    scratch = [
        pltpu.VMEM((N, N), jnp.bfloat16),
        ext_rows,
        ext_rows,
        ext_rows,
        strip_rows,
        full_state,
        full_state,
        *[strip_state] * 6,
        many(4, 2, ROWS, LANES),
        many(4, 2, M, 8, LANES),
        strip_rows,
        full_rows,
        strip_rows,
        strip_rows,
        strip_state,
        many(STAGE, 2, ROWS, LANES),
        many(STAGE + 1, 2, M, 8, LANES),
        strip_rows,
        strip_rows,
        strip_rows,
        strip_rows,
        strip_state,
        many(4, 2, ROWS, LANES),
        full_rows,
        dma((4,)),
        dma((4,)),
        dma((3,)),
        dma((4,)),
        dma,
        dma,
        dma((8,)),
        dma((STAGE,)),
        dma((4,)),
        dma((4,)),
        dma,
        dma,
        dma((4,)),
        dma((4,)),
    ]
    block = jax.ShapeDtypeStruct((1, N, N), F32)
    return pl.pallas_call(
        kernel,
        out_shape=(block, block),
        in_specs=[vmem] * 3,
        out_specs=(vmem, vmem),
        scratch_shapes=scratch,
        compiler_params=pltpu.CompilerParams(
            collective_id=0, has_side_effects=True, vmem_limit_bytes=32 * 2**20
        ),
    )(init_field, reaction, guesses)


def solution(mesh):
    return jax.shard_map(
        local,
        mesh=mesh,
        in_specs=(P(), P(), P(("tm", "grp"), None, None)),
        out_specs=(P(("tm", "grp"), None, None), P("tm", None, None)),
        check_vma=False,
    )
```

time: 461 us -> 53.2 us (0.12); the launches traced: 454 us -> 53 us
  waiting for transfers between devices: 294 us -> 0 us
  starting transfers between devices: 80.9 us -> 0 us
  Pallas kernels: 0 us -> 48.1 us
  local copies, waits for them, and re-layouts: 37.5 us -> 4.25 us
  other arithmetic: 22.8 us -> 0 us
  between operations: 14.6 us -> 0.65 us
    ppermute x35 -> x0, waiting for transfers between devices: 248 us -> none  [passed_along(): return lax.ppermute(block, axis, route)]
    ppermute x35 -> x0, starting transfers between devices: 80.9 us -> none  [passed_along(): return lax.ppermute(block, axis, route)]
    pallas_call x0 -> x1, Pallas kernels: none -> 48.1 us  [local(): pl.pallas_call(kernel, out_shape=(block, block), in_specs=[vmem] * 3, out...]
    all_gather x2 -> x0, waiting for transfers between devices: 46.3 us -> none  [the longest x1 24.3 us: local(): lax.all_gather(term[None], 'grp', axis=0, tiled=True)]
    slice x305 -> x0, local copies, waits for them, and re-layouts: 22.2 us -> none  [the longest x150 17.8 us: advance(): jnp.roll(values, -1, -1)]
    add x73 -> x0, other arithmetic: 17.8 us -> none  [the longest x32 8.22 us: advance(): values + factor * (KAPPA * (beside - 4.0 * values) + reaction * (values -...]
    while x64 -> x0, local copies, waits for them, and re-layouts: 12.9 us -> none
  transfers between devices with their start and end apart: 37 -> 0, of which waited for: 36 -> 0; matrix products, arithmetic and copies ran while one was open for 0% -> 0% of each run, Pallas kernels for 0% -> 0%
where the time goes in v1:
time: 53.2 us; the launch traced here: 53 us
  Pallas kernels  48.1 us (90%)
  local copies, waits for them, and re-layouts  4.25 us (8%)
  between operations  0.65 us (1%)
    pallas_call x1, Pallas kernels, local(): pl.pallas_call(kernel, out_shape=(block, block), in_specs=[vmem] * 3, out...  48.1 us
    unnamed x8, local copies, waits for them, and re-layouts  4.25 us

profile of v1, /device:TPU:5, one launch (start us, length us, event | category | flops | bytes accessed | tf_op | source)
XLA Modules:
  0.0 53.0 jit_solution(10173971406927972868)
XLA Ops:
  0.6 0.0 copy-start
  0.6 0.9 %copy-done = f32[256,256]{1,0:T(8,128)S(1)} copy-done((f32[256,256]{1,0:T(8,128)S(1)}, f32[256,256]{1,0:T(8,128)}, u32[]{:S(2)}) %copy-start) | copy-done | bytes 262168
  1.6 0.0 copy-start.1
  1.6 0.9 %copy-done.1 = f32[256,256]{1,0:T(8,128)S(1)} copy-done((f32[256,256]{1,0:T(8,128)S(1)}, f32[256,256]{1,0:T(8,128)}, u32[]{:S(2)}) %copy-start.1) | copy-done | bytes 262168
  2.5 0.0 copy-start.2
  2.5 0.9 %copy-done.2 = f32[1,256,256]{2,1,0:T(8,128)S(1)} copy-done((f32[1,256,256]{2,1,0:T(8,128)S(1)}, f32[1,256,256]{2,1,0:T(8,128)}, u32[]{:S(2)}) %copy-start.2) | copy-done | bytes 262168
  3.5 48.1 %shard_map.50 = (f32[1,256,256]{2,1,0:T(8,128)S(1)}, f32[1,256,256]{2,1,0:T(8,128)S(1)}) custom-call(f32[256,256]{1,0:T(8,128)S(1)} %copy-done, f32[256,256]{1,0:T(8,128)S(1)} %copy-done.1, f32[1,256,256]{2,1,0:T(8,128)S(1)} %copy-done.2), custom_call_target="tpu_custom_call" | custom-call | tf_op jit(solution)/shard_map/pallas_call | solution.py:566
  51.6 0.7 %copy.7 = f32[1,256,256]{2,1,0:T(8,128)} copy(f32[1,256,256]{2,1,0:T(8,128)S(1)} %get-tuple-element.4) | data formatting | bytes 524288
  52.3 0.7 %copy.8 = f32[1,256,256]{2,1,0:T(8,128)} copy(f32[1,256,256]{2,1,0:T(8,128)S(1)} %get-tuple-element.5) | data formatting | bytes 524288
Async XLA Ops:
  0.6 1.0 %copy-start = (f32[256,256]{1,0:T(8,128)S(1)}, f32[256,256]{1,0:T(8,128)}, u32[]{:S(2)}) copy-start(f32[256,256]{1,0:T(8,128)} %init_ref.1) | copy-start | bytes 786436
  1.6 0.9 %copy-start.1 = (f32[256,256]{1,0:T(8,128)S(1)}, f32[256,256]{1,0:T(8,128)}, u32[]{:S(2)}) copy-start(f32[256,256]{1,0:T(8,128)} %rate_ref.1) | copy-start | bytes 786436
  2.5 0.9 %copy-start.2 = (f32[1,256,256]{2,1,0:T(8,128)S(1)}, f32[1,256,256]{2,1,0:T(8,128)}, u32[]{:S(2)}) copy-start(f32[1,256,256]{2,1,0:T(8,128)} %guess_ref.1) | copy-start | bytes 786436

commit v2 on v1

--- a/solution.py
+++ b/solution.py
@@ -121,8 +121,11 @@
     init_ref,
     rate_ref,
     guess_ref,
-    points_ref,
+    points_full,
     corner_ref,
+    init_in,
+    rate_in,
+    prior_in,
     perm,
     init_ext,
     rate_ext,
@@ -151,7 +154,7 @@
     z_in,
     z_own,
     point_rows,
-    points_full,
+    in_sem,
     start_send,
     start_recv,
     corner_send,
@@ -179,6 +182,18 @@
     def around(distance):
         return (member + distance) % 4
 
+    first = jnp.logical_and(group == 0, member == 0)
+    rate_copy = pltpu.make_async_copy(rate_ref, rate_in, in_sem.at[0])
+    rate_copy.start()
+    prior_copies = (
+        pltpu.make_async_copy(init_ref, prior_in, in_sem.at[1]),
+        pltpu.make_async_copy(guess_ref.at[0], prior_in, in_sem.at[1]),
+    )
+    pl.when(first)(prior_copies[0].start)
+    pl.when(jnp.logical_not(first))(prior_copies[1].start)
+    init_copy = pltpu.make_async_copy(init_ref, init_in, in_sem.at[2])
+    init_copy.start()
+
     barrier = pltpu.get_barrier_semaphore()
 
     def greet(tm, grp):
@@ -220,11 +235,13 @@
     )
 
     perm[...] = permutation(False)
-    rate = permuted(rate_ref[...], perm[...])
+    rate_copy.wait()
+    rate = permuted(rate_in[...], perm[...])
     widen(rate_ext, rate)
-    first = jnp.logical_and(group == 0, member == 0)
-    prior = jnp.where(first, init_ref[...], guess_ref[0])
-    widen(relaxed_ext, permuted(prior, perm[...]))
+    prior_copies[1].wait()
+    prior = permuted(prior_in[...], perm[...])
+    for h in range(2):
+        relaxed_ext[h, HALO : HALO + N] = prior[:, h * LANES : (h + 1) * LANES]
     full = relaxed_ext.at[:, HALO : HALO + N]
     rates = load_rows(rate_ext.at[:, HALO : HALO + N], MF)
     for h in range(2):
@@ -263,7 +280,8 @@
     def _():
         copy_strip(starts.at[slot], relaxed_ext, own_first)
 
-    widen(init_ext, permuted(init_ref[...], perm[...]))
+    init_copy.wait()
+    widen(init_ext, permuted(init_in[...], perm[...]))
 
     @pl.when(group == 0)
     def _():
@@ -285,29 +303,40 @@
     copy_strip(strip, init_ext, own_first)
     perm[...] = permutation(True)
 
-    def one_term(turn, _):
-        offset = turn + (turn == 2).astype(jnp.int32) - (turn == 3).astype(jnp.int32)
-        s = (member + 1 + offset) % 4
-        remote = jnp.where(s == 0, group > 0, s != member + 1)
-
-        @pl.when(remote)
-        def _():
-            pltpu.make_async_remote_copy(
-                src_ref=starts.at[s],
-                dst_ref=starts.at[s],
-                send_sem=start_send.at[0],
-                recv_sem=start_recv.at[s],
-                device_id=(group, around(1)),
-                device_id_type=MESH,
-            ).wait_recv()
-
-        start = load_rows(starts.at[s], M)
-        store_state(terms.at[s], advance(start, a_16, b_16, 16.0 * KAPPA))
-        fine = repeat(load_rows(starts.at[s], M), a_1, b_1, KAPPA, STEPS, 4)
-        store_state(terms.at[s], minus(fine, load_state(terms.at[s])))
-        return 0
-
-    lax.fori_loop(0, 4, one_term, 0)
+    def make_terms(slots):
+        for s in slots:
+            remote = jnp.where(s == 0, group > 0, s != member + 1)
+
+            @pl.when(remote)
+            def _(s=s):
+                pltpu.make_async_remote_copy(
+                    src_ref=starts.at[s],
+                    dst_ref=starts.at[s],
+                    send_sem=start_send.at[0],
+                    recv_sem=start_recv.at[s],
+                    device_id=(group, around(1)),
+                    device_id_type=MESH,
+                ).wait_recv()
+
+        for s in slots:
+            start = load_rows(starts.at[s], M)
+            store_state(terms.at[s], advance(start, a_16, b_16, 16.0 * KAPPA))
+
+        def turn(_, carried):
+            for _ in range(4):
+                carried = [advance(state, a_1, b_1, KAPPA) for state in carried]
+            return tuple(tuple(tuple(half) for half in state) for state in carried)
+
+        carried = tuple(
+            tuple(tuple(half) for half in load_rows(starts.at[s], M)) for s in slots
+        )
+        fine = lax.fori_loop(0, STEPS // 4, turn, carried)
+        for s, state in zip(slots, fine):
+            store_state(terms.at[s], minus(state, load_state(terms.at[s])))
+
+    make_terms([slot])
+    make_terms([(slot + 1) % 4, (slot + 3) % 4])
+    make_terms([(slot + 2) % 4])
 
     def big_step(state, index):
         stepped = advance(state, a_16, b_16, 16.0 * KAPPA)
@@ -352,23 +381,37 @@
     state = minus(state, advance(load_rows(fresh, M), a_64, b_64, 64.0 * KAPPA))
     store_state(ct, state)
     store_rows(ct_rows, state)
-    for dx in (1, 0):
-        for dy in (2, 1, 3, 0):
-            px, py = stage * 2 + (chip_x + dx) % 2, (y + dy) % 4
-            copy = pltpu.make_async_remote_copy(
-                src_ref=ct_rows.at[:, sent],
-                dst_ref=cts.at[local_group, :, sent],
-                send_sem=ct_send.at[dx * 4 + dy],
-                recv_sem=ct_recv.at[local_group],
-                device_id=(at_xy(px, py, 0), member),
-                device_id_type=MESH,
-            )
-            when = None if (dx, dy) != (0, 0) else c == 1
-            if when is None:
+    def ct_copies(halo):
+        rows = slice(HALO - halo, HALO + CORE + halo)
+        copies = []
+        for dx in (1, 0):
+            for dy in (2, 1, 3, 0):
+                px, py = stage * 2 + (chip_x + dx) % 2, (y + dy) % 4
+                copies.append(
+                    pltpu.make_async_remote_copy(
+                        src_ref=ct_rows.at[:, rows],
+                        dst_ref=cts.at[local_group, :, rows],
+                        send_sem=ct_send.at[dx * 4 + dy],
+                        recv_sem=ct_recv.at[local_group],
+                        device_id=(at_xy(px, py, 0), member),
+                        device_id_type=MESH,
+                    )
+                )
+        return copies
+
+    widths = (
+        (24, local_group == 0),
+        (16, jnp.logical_and(local_group > 0, local_group <= 8)),
+        (8, local_group > 8),
+    )
+    for halo, when in widths:
+
+        @pl.when(when)
+        def _(halo=halo):
+            copies = ct_copies(halo)
+            for copy in copies[:-1]:
                 copy.start()
-            else:
-                pl.when(when)(copy.start)
-            pending.append((when, copy))
+            pl.when(c == 1)(copies[-1].start)
 
     for d in (1, 3, 2):
         q = around(d)
@@ -381,7 +424,7 @@
             device_id_type=MESH,
         ).wait_recv()
     both = jnp.concatenate([corner_full[0], corner_full[1]], axis=1)
-    corner_ref[0] = permuted(both, perm[...])
+    corner_ref[...] = permuted(both, perm[...])
 
     hop = []
     rows = 24
@@ -425,26 +468,27 @@
                 copy.wait_recv()
             store_state(history.at[0], load_rows(z_stage, M))
 
-        def one_group(t, state):
-            @pl.when(t != local_group)
-            def _():
-                pltpu.make_async_remote_copy(
-                    src_ref=ct_rows.at[:, sent],
-                    dst_ref=cts.at[t, :, sent],
-                    send_sem=ct_send.at[0],
-                    recv_sem=ct_recv.at[t],
-                    device_id=(group, around(1)),
-                    device_id_type=MESH,
-                ).wait_recv()
-
-            state = [list(half) for half in state]
-            state = advance(state, a_64, b_64, 64.0 * KAPPA)
-            state = plus(state, load_rows(cts.at[t], M))
-            store_state(history.at[t + 1], state)
-            return tuple(tuple(half) for half in state)
-
-        begin = tuple(tuple(half) for half in load_state(history.at[0]))
-        last = lax.fori_loop(0, STAGE, one_group, begin)
+        last = load_state(history.at[0])
+        for t in range(STAGE):
+            if t % 4 == 0:
+                for n in range(t, t + 4):
+                    halo = 24 if n == 0 else 16 if n <= 8 else 8
+                    rows = slice(HALO - halo, HALO + CORE + halo)
+
+                    @pl.when(n != local_group)
+                    def _(n=n, rows=rows):
+                        pltpu.make_async_remote_copy(
+                            src_ref=ct_rows.at[:, rows],
+                            dst_ref=cts.at[n, :, rows],
+                            send_sem=ct_send.at[0],
+                            recv_sem=ct_recv.at[n],
+                            device_id=(group, around(1)),
+                            device_id_type=MESH,
+                        ).wait_recv()
+
+            last = advance(last, a_64, b_64, 64.0 * KAPPA)
+            last = plus(last, load_rows(cts.at[t], M))
+            store_state(history.at[t + 1], last)
 
         @pl.when(stage == 0)
         def _():
@@ -464,9 +508,10 @@
     final = load_state(z_own)
     final = plus(advance(final, a_64, b_64, 64.0 * KAPPA), load_state(ct))
     state = load_state(z_own)
-    for index in range(4):
-        state = big_step(state, index) if index < 3 else final
-        store_rows(point_rows.at[index], state)
+    for index in (3, 0, 1, 2):
+        if index < 3:
+            state = big_step(state, index)
+        store_rows(point_rows.at[index], state if index < 3 else final)
 
         copy = pltpu.make_async_remote_copy(
             src_ref=point_rows.at[index, :, core_rows],
@@ -491,8 +536,6 @@
             device_id=(group, q),
             device_id_type=MESH,
         ).wait_recv()
-    both = jnp.concatenate([points_full[0], points_full[1]], axis=1)
-    points_ref[0] = permuted(both, perm[...])
 
     for when, copy in pending:
         if when is None:
@@ -500,6 +543,15 @@
         else:
             pl.when(when)(copy.wait_send)
 
+    for halo, when in widths:
+
+        @pl.when(when)
+        def _(halo=halo):
+            copies = ct_copies(halo)
+            for copy in copies[:-1]:
+                copy.wait_send()
+            pl.when(c == 1)(copies[-1].wait_send)
+
     @pl.when(core0)
     def _():
         pass_copy.wait_send()
@@ -508,6 +560,24 @@
         def _():
             for copy in hop:
                 copy.wait_send()
+
+
+def write_out(points_full, corner, points_out, corner_out, rows, sems):
+    corner_copy = pltpu.make_async_copy(corner, corner_out.at[0], sems.at[0])
+    corner_copy.start()
+    matrix = permutation(True)
+    copies = [corner_copy]
+    for part in range(2):
+        some = slice(part * LANES, (part + 1) * LANES)
+        both = jnp.concatenate([points_full[0, some], points_full[1, some]], axis=1)
+        rows[some] = permuted(both, matrix)
+        copy = pltpu.make_async_copy(
+            rows.at[some], points_out.at[0, some], sems.at[1 + part]
+        )
+        copy.start()
+        copies.append(copy)
+    for copy in copies:
+        copy.wait()
 
 
 def local(init_field, reaction, guesses):
@@ -523,6 +593,7 @@
         return pltpu.VMEM((count, *shape), F32)
 
     scratch = [
+        *[pltpu.VMEM((N, N), F32)] * 3,
         pltpu.VMEM((N, N), jnp.bfloat16),
         ext_rows,
         ext_rows,
@@ -546,7 +617,7 @@
         strip_rows,
         strip_state,
         many(4, 2, ROWS, LANES),
-        full_rows,
+        dma((3,)),
         dma((4,)),
         dma((4,)),
         dma((3,)),
@@ -562,17 +633,29 @@
         dma((4,)),
         dma((4,)),
     ]
-    block = jax.ShapeDtypeStruct((1, N, N), F32)
-    return pl.pallas_call(
+    hbm = pl.BlockSpec(memory_space=pltpu.HBM)
+    points, corner = pl.pallas_call(
         kernel,
-        out_shape=(block, block),
-        in_specs=[vmem] * 3,
+        out_shape=(
+            jax.ShapeDtypeStruct((2, N, LANES), F32),
+            jax.ShapeDtypeStruct((N, N), F32),
+        ),
+        in_specs=[hbm] * 3,
         out_specs=(vmem, vmem),
         scratch_shapes=scratch,
         compiler_params=pltpu.CompilerParams(
-            collective_id=0, has_side_effects=True, vmem_limit_bytes=32 * 2**20
+            collective_id=0, has_side_effects=True, vmem_limit_bytes=213 * 2**18
         ),
     )(init_field, reaction, guesses)
+    block = jax.ShapeDtypeStruct((1, N, N), F32)
+    return pl.pallas_call(
+        write_out,
+        out_shape=(block, block),
+        in_specs=[vmem] * 2,
+        out_specs=(hbm, hbm),
+        scratch_shapes=[pltpu.VMEM((N, N), F32), dma((3,))],
+        compiler_params=pltpu.CompilerParams(vmem_limit_bytes=8 * 2**20),
+    )(points, corner)
 
 
 def solution(mesh):

time: 53.2 us -> 47.7 us (0.90)
  local copies, waits for them, and re-layouts: 4.25 us -> 0 us
  Pallas kernels: 48.1 us -> 46.9 us
    unnamed x8 -> x0, local copies, waits for them, and re-layouts: 4.25 us -> none
    pallas_call x1 -> x2, Pallas kernels: 48.1 us -> 46.9 us  [the longest x1 45.9 us: local(): pl.pallas_call(kernel, out_shape=(jax.ShapeDtypeStruct((2, N, LANES), F32...]
where the time goes in v2:
time: 47.7 us; the launch traced here: 47.5 us
  Pallas kernels  46.9 us (98%)
  between operations  0.64 us (1%)
    pallas_call x1, Pallas kernels, local(): pl.pallas_call(kernel, out_shape=(jax.ShapeDtypeStruct((2, N, LANES), F32...  45.9 us
    pallas_call x1, Pallas kernels, local(): pl.pallas_call(write_out, out_shape=(block, block), in_specs=[vmem] * 2,...  1.01 us

profile of v2, /device:TPU:5, one launch (start us, length us, event | category | flops | bytes accessed | tf_op | source)
XLA Modules:
  0.0 47.5 jit_solution(15757836594910031765)
XLA Ops:
  0.6 45.9 %shard_map.50 = (f32[2,256,128]{2,1,0:T(8,128)S(1)}, f32[256,256]{1,0:T(8,128)S(1)}) custom-call(f32[256,256]{1,0:T(8,128)} %init_ref.1, f32[256,256]{1,0:T(8,128)} %rate_ref.1, f32[1,256,256]{2,1,0:T(8,128)} %guess_ref.1), custom_call_target="tpu_custom_call" | custom-call | tf_op jit(solution)/shard_map/pallas_call | solution.py:637
  46.5 1.0 %shard_map.51 = (f32[1,256,256]{2,1,0:T(8,128)}, f32[1,256,256]{2,1,0:T(8,128)}) custom-call(f32[2,256,128]{2,1,0:T(8,128)S(1)} %get-tuple-element.4.points_full, f32[256,256]{1,0:T(8,128)S(1)} %get-tuple-element.5.corner), custom_call_target="tpu_custom_call" | custom-call | tf_op jit(solution)/shard_map/pallas_call | solution.py:651

commit v3 on v2

--- a/solution.py
+++ b/solution.py
@@ -121,7 +121,7 @@
     init_ref,
     rate_ref,
     guess_ref,
-    points_full,
+    points_ref,
     corner_ref,
     init_in,
     rate_in,
@@ -154,9 +154,11 @@
     z_in,
     z_own,
     point_rows,
+    points_full,
     in_sem,
     start_send,
     start_recv,
+    forward_send,
     corner_send,
     corner_recv,
     fresh_send,
@@ -248,7 +250,7 @@
         for k in range(MF):
             a_full[h, k] = (1.0 - 4.0 * KAPPA) + rates[h][k]
             b_full[h, k] = rates[h][k]
-    relaxed = repeat(load_rows(full, MF), a_full, b_full, KAPPA, STEPS, 4)
+    relaxed = repeat(load_rows(full, MF), a_full, b_full, KAPPA, STEPS, 8)
     store_rows(relaxed_ext, relaxed, HALO)
     for h in range(2):
         relaxed_ext[h, 0:HALO] = relaxed_ext[h, N : N + HALO]
@@ -260,13 +262,21 @@
     slot = (member + 1) % 4
     target = group + (member == 3).astype(jnp.int32)
     have = jnp.logical_or(member < 3, group < groups - 1)
-    for d in (1, 3, 2, 0):
+    for d, part, low, high in (
+        (1, 0, CORE, ROWS),
+        (3, 0, 0, ROWS - CORE),
+        (1, 1, 0, CORE),
+        (3, 1, ROWS - CORE, ROWS),
+        (0, 0, 0, ROWS),
+    ):
         q = around(d)
         copy = pltpu.make_async_remote_copy(
-            src_ref=relaxed_ext.at[:, pl.ds(pl.multiple_of(q * CORE, 8), ROWS)],
-            dst_ref=starts.at[slot],
-            send_sem=start_send.at[d],
-            recv_sem=start_recv.at[slot],
+            src_ref=relaxed_ext.at[
+                :, pl.ds(pl.multiple_of(q * CORE + low, 8), high - low)
+            ],
+            dst_ref=starts.at[slot, :, low:high],
+            send_sem=start_send.at[2 * d + part if d else 0],
+            recv_sem=start_recv.at[slot, part],
             device_id=(target, q),
             device_id_type=MESH,
         )
@@ -303,40 +313,87 @@
     copy_strip(strip, init_ext, own_first)
     perm[...] = permutation(True)
 
+    def arrived(s, low, high, part):
+        pltpu.make_async_remote_copy(
+            src_ref=starts.at[s, :, low:high],
+            dst_ref=starts.at[s, :, low:high],
+            send_sem=start_send.at[0],
+            recv_sem=start_recv.at[s, part],
+            device_id=(group, around(1)),
+            device_id_type=MESH,
+        ).wait_recv()
+
     def make_terms(slots):
-        for s in slots:
-            remote = jnp.where(s == 0, group > 0, s != member + 1)
-
-            @pl.when(remote)
-            def _(s=s):
-                pltpu.make_async_remote_copy(
-                    src_ref=starts.at[s],
-                    dst_ref=starts.at[s],
-                    send_sem=start_send.at[0],
-                    recv_sem=start_recv.at[s],
-                    device_id=(group, around(1)),
-                    device_id_type=MESH,
-                ).wait_recv()
-
         for s in slots:
             start = load_rows(starts.at[s], M)
             store_state(terms.at[s], advance(start, a_16, b_16, 16.0 * KAPPA))
 
         def turn(_, carried):
-            for _ in range(4):
+            for _ in range(8):
                 carried = [advance(state, a_1, b_1, KAPPA) for state in carried]
             return tuple(tuple(tuple(half) for half in state) for state in carried)
 
         carried = tuple(
             tuple(tuple(half) for half in load_rows(starts.at[s], M)) for s in slots
         )
-        fine = lax.fori_loop(0, STEPS // 4, turn, carried)
+        fine = lax.fori_loop(0, STEPS // 8, turn, carried)
         for s, state in zip(slots, fine):
             store_state(terms.at[s], minus(state, load_state(terms.at[s])))
 
-    make_terms([slot])
-    make_terms([(slot + 1) % 4, (slot + 3) % 4])
-    make_terms([(slot + 2) % 4])
+    below, above, far = (slot + 3) % 4, (slot + 1) % 4, (slot + 2) % 4
+
+    def there(s):
+        return jnp.logical_or(s != 0, group > 0)
+
+    @pl.when(member < 3)
+    def _():
+        make_terms([slot])
+
+    half = ROWS // 2
+    for s, part, low, to, to_low, d in (
+        (below, 0, CORE, 0, 0, 1),
+        (above, 0, 8, 1, half, 3),
+    ):
+        copy = pltpu.make_async_remote_copy(
+            src_ref=starts.at[s, :, low : low + half],
+            dst_ref=starts.at[s, :, to_low : to_low + half],
+            send_sem=forward_send.at[to],
+            recv_sem=start_recv.at[s, to],
+            device_id=(group, around(d)),
+            device_id_type=MESH,
+        )
+
+        @pl.when(there(s))
+        def _(s=s, d=d, copy=copy):
+            arrived(s, *((CORE, ROWS) if d == 1 else (0, ROWS - CORE)), 0)
+            copy.start()
+
+        pending.append((there(s), copy))
+
+    @pl.when(member == 3)
+    def _():
+        @pl.when(group > 0)
+        def _():
+            arrived(slot, 0, ROWS, 0)
+
+        make_terms([slot])
+
+    @pl.when(there(below))
+    def _():
+        arrived(below, 0, CORE, 1)
+
+    @pl.when(there(above))
+    def _():
+        arrived(above, ROWS - CORE, ROWS, 1)
+
+    make_terms([below, above])
+
+    @pl.when(there(far))
+    def _():
+        arrived(far, 0, half, 0)
+        arrived(far, half, ROWS, 1)
+
+    make_terms([far])
 
     def big_step(state, index):
         stepped = advance(state, a_16, b_16, 16.0 * KAPPA)
@@ -347,17 +404,19 @@
         corner = big_step(corner, index)
     store_rows(corner_rows, corner)
     sent = slice(HALO - 24, HALO + CORE + 24)
-    copy = pltpu.make_async_remote_copy(
-        src_ref=corner_rows.at[:, sent],
-        dst_ref=fresh.at[:, sent],
-        send_sem=fresh_send,
-        recv_sem=fresh_recv,
-        device_id=(lax.rem(group + 1, groups), member),
-        device_id_type=MESH,
-    )
-    fresh_copy = copy
-    pl.when(group < groups - 1)(copy.start)
-    pending.append((group < groups - 1, copy))
+    fresh_copies = []
+    for h in range(1):
+        copy = pltpu.make_async_remote_copy(
+            src_ref=corner_rows.at[:, sent],
+            dst_ref=fresh.at[:, sent],
+            send_sem=fresh_send.at[h],
+            recv_sem=fresh_recv.at[h],
+            device_id=(lax.rem(group + 1, groups), member),
+            device_id_type=MESH,
+        )
+        fresh_copies.append(copy)
+        pl.when(group < groups - 1)(copy.start)
+        pending.append((group < groups - 1, copy))
     core_rows = slice(HALO, HALO + CORE)
     own_rows = pl.ds(own_first, CORE)
     for d in (1, 3, 2):
@@ -374,7 +433,8 @@
     for h in range(2):
         corner_full[h, own_rows] = corner_rows[h, core_rows]
 
-    pl.when(group > 0)(fresh_copy.wait_recv)
+    for copy in fresh_copies:
+        pl.when(group > 0)(copy.wait_recv)
     state = load_rows(fresh, M)
     for index in range(4):
         state = big_step(state, index)
@@ -526,16 +586,20 @@
         pending.append((when, copy))
     for h in range(2):
         points_full[h, own_rows] = point_rows[member, h, core_rows]
-    for d in (1, 3, 2):
+    for d in (0, 1, 3, 2):
         q = around(d)
-        pltpu.make_async_remote_copy(
-            src_ref=point_rows.at[0, :, core_rows],
-            dst_ref=points_full.at[:, pl.ds(pl.multiple_of(q * CORE, 8), CORE)],
-            send_sem=point_send.at[0],
-            recv_sem=point_recv.at[q],
-            device_id=(group, q),
-            device_id_type=MESH,
-        ).wait_recv()
+        rows = pl.ds(pl.multiple_of(q * CORE, 8), CORE)
+        if d:
+            pltpu.make_async_remote_copy(
+                src_ref=point_rows.at[0, :, core_rows],
+                dst_ref=points_full.at[:, rows],
+                send_sem=point_send.at[0],
+                recv_sem=point_recv.at[q],
+                device_id=(group, q),
+                device_id_type=MESH,
+            ).wait_recv()
+        both = jnp.concatenate([points_full[0, rows], points_full[1, rows]], axis=1)
+        points_ref[rows] = permuted(both, perm[...])
 
     for when, copy in pending:
         if when is None:
@@ -562,20 +626,13 @@
                 copy.wait_send()
 
 
-def write_out(points_full, corner, points_out, corner_out, rows, sems):
-    corner_copy = pltpu.make_async_copy(corner, corner_out.at[0], sems.at[0])
-    corner_copy.start()
-    matrix = permutation(True)
-    copies = [corner_copy]
-    for part in range(2):
-        some = slice(part * LANES, (part + 1) * LANES)
-        both = jnp.concatenate([points_full[0, some], points_full[1, some]], axis=1)
-        rows[some] = permuted(both, matrix)
-        copy = pltpu.make_async_copy(
-            rows.at[some], points_out.at[0, some], sems.at[1 + part]
-        )
+def write_out(points, corner, points_out, corner_out, sems):
+    copies = (
+        pltpu.make_async_copy(points, points_out.at[0], sems.at[0]),
+        pltpu.make_async_copy(corner, corner_out.at[0], sems.at[1]),
+    )
+    for copy in copies:
         copy.start()
-        copies.append(copy)
     for copy in copies:
         copy.wait()
 
@@ -617,13 +674,15 @@
         strip_rows,
         strip_state,
         many(4, 2, ROWS, LANES),
+        full_rows,
+        dma((3,)),
+        dma((8,)),
+        dma((4, 2)),
+        dma((2,)),
         dma((3,)),
         dma((4,)),
-        dma((4,)),
-        dma((3,)),
-        dma((4,)),
-        dma,
-        dma,
+        dma((2,)),
+        dma((2,)),
         dma((8,)),
         dma((STAGE,)),
         dma((4,)),
@@ -637,7 +696,7 @@
     points, corner = pl.pallas_call(
         kernel,
         out_shape=(
-            jax.ShapeDtypeStruct((2, N, LANES), F32),
+            jax.ShapeDtypeStruct((N, N), F32),
             jax.ShapeDtypeStruct((N, N), F32),
         ),
         in_specs=[hbm] * 3,
@@ -653,7 +712,7 @@
         out_shape=(block, block),
         in_specs=[vmem] * 2,
         out_specs=(hbm, hbm),
-        scratch_shapes=[pltpu.VMEM((N, N), F32), dma((3,))],
+        scratch_shapes=[dma((2,))],
         compiler_params=pltpu.CompilerParams(vmem_limit_bytes=8 * 2**20),
     )(points, corner)
 

time: 47.7 us -> 46.1 us (0.966)
  Pallas kernels: 46.9 us -> 45.1 us
    pallas_call x1, Pallas kernels: 45.9 us -> 44.3 us  [local(): pl.pallas_call(kernel, out_shape=(jax.ShapeDtypeStruct((N, N), F32), jax....]
where the time goes in v3:
time: 46.1 us; the launch traced here: 45.8 us
  Pallas kernels  45.1 us (98%)
  between operations  0.64 us (1%)
    pallas_call x1, Pallas kernels, local(): pl.pallas_call(kernel, out_shape=(jax.ShapeDtypeStruct((N, N), F32), jax....  44.3 us

profile of v3, /device:TPU:5, one launch (start us, length us, event | category | flops | bytes accessed | tf_op | source)
XLA Modules:
  0.0 45.8 jit_solution(16077134244803064394)
XLA Ops:
  0.6 44.3 %shard_map.50 = (f32[256,256]{1,0:T(8,128)S(1)}, f32[256,256]{1,0:T(8,128)S(1)}) custom-call(f32[256,256]{1,0:T(8,128)} %init_ref.1, f32[256,256]{1,0:T(8,128)} %rate_ref.1, f32[1,256,256]{2,1,0:T(8,128)} %guess_ref.1), custom_call_target="tpu_custom_call" | custom-call | tf_op jit(solution)/shard_map/pallas_call | solution.py:696
  45.0 0.8 %shard_map.51 = (f32[1,256,256]{2,1,0:T(8,128)}, f32[1,256,256]{2,1,0:T(8,128)}) custom-call(f32[256,256]{1,0:T(8,128)S(1)} %get-tuple-element.4.points, f32[256,256]{1,0:T(8,128)S(1)} %get-tuple-element.5.corner), custom_call_target="tpu_custom_call" | custom-call | tf_op jit(solution)/shard_map/pallas_call | solution.py:710

commit v4 on v3

--- a/solution.py
+++ b/solution.py
@@ -19,6 +19,10 @@
 M = ROWS // 8
 MF = N // 8
 STAGE = 16
+HALF = CORE // 2
+EDGE = 24
+HALF_ROWS = HALF + 2 * EDGE
+MH = HALF_ROWS // 8
 F32 = jnp.float32
 
 
@@ -110,9 +114,9 @@
         ext[h, HALO + N :] = part[:HALO]
 
 
-def copy_strip(dst, ext, first):
-    for h in range(2):
-        for row in range(0, ROWS, 8):
+def copy_strip(dst, ext, first, rows=ROWS):
+    for h in range(2):
+        for row in range(0, rows, 8):
             src = pl.ds(pl.multiple_of(first + row, 8), 8)
             dst[h, row : row + 8] = ext[h, src]
 
@@ -148,6 +152,10 @@
     ct,
     cts,
     history,
+    half_history,
+    half_strip,
+    a_half,
+    b_half,
     hop_rows,
     z_stage,
     pass_rows,
@@ -180,6 +188,8 @@
     chip_x = x % 2
     local_group = group % STAGE
     core0 = c == 0
+    mine = (x + y) % 2
+    half_first = HALO - EDGE + HALF * mine
 
     def around(distance):
         return (member + distance) % 4
@@ -220,12 +230,18 @@
 
     @pl.when(jnp.logical_and(core0, stage == 1))
     def _():
-        for d in (0, 1, 3):
-            greet(at_xy(3 - x, y, 0), around(d))
+        for dy in (0, 3):
+            py = (y + dy) % 4
+            greet(at_xy(3 - x, py, 0), member)
+            greet(at_xy(3 - x, py, 0), around(1 + 2 * ((3 - x + py) % 2)))
 
     @pl.when(c == 1)
     def _():
         greet(group - 1, member)
+
+    @pl.when(stage == 0)
+    def _():
+        greet(at_xy(1 - x, y, 0), member)
 
     more = (group < groups - 1).astype(jnp.int32)
     expected = (
@@ -233,7 +249,7 @@
         + more * (1 + 4 * (member == 3).astype(jnp.int32))
         + 7
         + c
-        + (1 - c) * (1 + 3 * (1 - stage))
+        + (1 - c) * (1 + 6 * (1 - stage))
     )
 
     perm[...] = permutation(False)
@@ -313,6 +329,18 @@
     copy_strip(strip, init_ext, own_first)
     perm[...] = permutation(True)
 
+    @pl.when(jnp.logical_and(core0, stage == 0))
+    def _():
+        first_row = own_first + half_first
+        copy_strip(half_strip, rate_ext, first_row, HALF_ROWS)
+        rates = load_rows(half_strip, MH)
+        for h in range(2):
+            for k in range(MH):
+                r = 64.0 * rates[h][k]
+                a_half[h, k] = (1.0 - 4.0 * KAPPA * 64.0) + r
+                b_half[h, k] = r
+        copy_strip(half_strip, init_ext, first_row, HALF_ROWS)
+
     def arrived(s, low, high, part):
         pltpu.make_async_remote_copy(
             src_ref=starts.at[s, :, low:high],
@@ -441,16 +469,21 @@
     state = minus(state, advance(load_rows(fresh, M), a_64, b_64, 64.0 * KAPPA))
     store_state(ct, state)
     store_rows(ct_rows, state)
-    def ct_copies(halo):
-        rows = slice(HALO - halo, HALO + CORE + halo)
+    def ct_copies(halo, of_stage):
         copies = []
         for dx in (1, 0):
             for dy in (2, 1, 3, 0):
-                px, py = stage * 2 + (chip_x + dx) % 2, (y + dy) % 4
+                px, py = of_stage * 2 + (chip_x + dx) % 2, (y + dy) % 4
+                if of_stage:
+                    src = dst = slice(HALO - halo, HALO + CORE + halo)
+                else:
+                    its_first = HALO - halo + HALF * ((px + py) % 2)
+                    src = pl.ds(pl.multiple_of(its_first, 8), HALF + 2 * halo)
+                    dst = slice(EDGE - halo, EDGE + HALF + halo)
                 copies.append(
                     pltpu.make_async_remote_copy(
-                        src_ref=ct_rows.at[:, rows],
-                        dst_ref=cts.at[local_group, :, rows],
+                        src_ref=ct_rows.at[:, src],
+                        dst_ref=cts.at[local_group, :, dst],
                         send_sem=ct_send.at[dx * 4 + dy],
                         recv_sem=ct_recv.at[local_group],
                         device_id=(at_xy(px, py, 0), member),
@@ -465,13 +498,14 @@
         (8, local_group > 8),
     )
     for halo, when in widths:
-
-        @pl.when(when)
-        def _(halo=halo):
-            copies = ct_copies(halo)
-            for copy in copies[:-1]:
-                copy.start()
-            pl.when(c == 1)(copies[-1].start)
+        for of_stage in range(2):
+
+            @pl.when(jnp.logical_and(when, stage == of_stage))
+            def _(halo=halo, of_stage=of_stage):
+                copies = ct_copies(halo, of_stage)
+                for copy in copies[:-1]:
+                    copy.start()
+                pl.when(c == 1)(copies[-1].start)
 
     for d in (1, 3, 2):
         q = around(d)
@@ -486,81 +520,140 @@
     both = jnp.concatenate([corner_full[0], corner_full[1]], axis=1)
     corner_ref[...] = permuted(both, perm[...])
 
+    def remote(src, dst, send, recv, tm, grp=member):
+        return pltpu.make_async_remote_copy(
+            src_ref=src,
+            dst_ref=dst,
+            send_sem=send,
+            recv_sem=recv,
+            device_id=(tm, grp),
+            device_id_type=MESH,
+        )
+
+    def rows_at(first, count):
+        return pl.ds(pl.multiple_of(first, 8), count)
+
     hop = []
-    rows = 24
-    for d, src, dst in (
-        (3, HALO, HALO + CORE),
-        (1, HALO + CORE - rows, HALO - rows),
-        (0, HALO, HALO),
+    for dy in (1, 0):
+        tm = at_xy(3 - x, (y + dy) % 4, 0)
+        hop.append(
+            remote(
+                hop_rows.at[:, rows_at(EDGE + 8 * mine, EDGE)],
+                z_stage.at[:, rows_at(HALO + CORE - (CORE + EDGE) * mine, EDGE)],
+                hop_send.at[2 * dy],
+                hop_recv.at[2 + mine],
+                tm,
+                around(3 - 2 * mine),
+            )
+        )
+        hop.append(
+            remote(
+                hop_rows.at[:, EDGE : EDGE + HALF],
+                z_stage.at[:, rows_at(HALO + HALF * mine, HALF)],
+                hop_send.at[2 * dy + 1],
+                hop_recv.at[mine],
+                tm,
+            )
+        )
+    hop_arrivals = []
+    for n, (first, count) in enumerate(
+        (
+            (HALO, HALF),
+            (HALO + HALF, HALF),
+            (HALO + CORE, EDGE),
+            (HALO - EDGE, EDGE),
+        )
     ):
-        count = rows if d else CORE
-        hop.append(
-            pltpu.make_async_remote_copy(
-                src_ref=hop_rows.at[:, src : src + count],
-                dst_ref=z_stage.at[:, dst : dst + count],
-                send_sem=hop_send.at[d],
-                recv_sem=hop_recv.at[d],
-                device_id=(at_xy(3 - x, y, 0), around(d)),
-                device_id_type=MESH,
+        there_rows = z_stage.at[:, first : first + count]
+        hop_arrivals.append(
+            remote(there_rows, there_rows, hop_send.at[0], hop_recv.at[n], group)
+        )
+
+    handed = slice(HALO - 8, HALO + CORE + 8)
+    sibling = at_xy(x, y, 1)
+    pass_copy = remote(
+        pass_rows.at[0, :, handed],
+        z_in.at[:, handed],
+        pass_send.at[0],
+        pass_recv.at[0],
+        sibling,
+    )
+    part = HALF + 8
+    half_src, half_dst = 16 + 8 * mine, HALO - 8 + part * mine
+    given = []
+    for n, tm in enumerate((sibling, at_xy(1 - x, y, 0), at_xy(1 - x, y, 1))):
+        given.append(
+            remote(
+                pass_rows.at[n, :, rows_at(half_src, part)],
+                z_in.at[:, rows_at(half_dst, part)],
+                pass_send.at[n],
+                pass_recv.at[mine],
+                tm,
             )
         )
-    handed = slice(HALO - 8, HALO + CORE + 8)
-    pass_copy = pltpu.make_async_remote_copy(
-        src_ref=pass_rows.at[:, handed],
-        dst_ref=z_in.at[:, handed],
-        send_sem=pass_send,
-        recv_sem=pass_recv,
-        device_id=(at_xy(x, y, 1), member),
-        device_id_type=MESH,
-    )
-
-    @pl.when(core0)
-    def _():
-        store_rows(cts.at[local_group], load_state(ct))
-
-        @pl.when(stage == 0)
-        def _():
-            store_state(history.at[0], load_rows(strip, M))
-
-        @pl.when(stage == 1)
-        def _():
-            for copy in hop:
-                copy.wait_recv()
-            store_state(history.at[0], load_rows(z_stage, M))
-
-        last = load_state(history.at[0])
+
+    def half_arrived(which):
+        there_rows = z_in.at[:, rows_at(HALO - 8 + part * which, part)]
+        remote(
+            there_rows, there_rows, pass_send.at[0], pass_recv.at[which], group
+        ).wait_recv()
+
+    def chain(begin, a_ref, b_ref, core, states, edge):
+        last = begin
+        m = len(begin[0])
         for t in range(STAGE):
             if t % 4 == 0:
                 for n in range(t, t + 4):
                     halo = 24 if n == 0 else 16 if n <= 8 else 8
-                    rows = slice(HALO - halo, HALO + CORE + halo)
+                    rows = cts.at[n, :, edge - halo : edge + core + halo]
 
                     @pl.when(n != local_group)
                     def _(n=n, rows=rows):
-                        pltpu.make_async_remote_copy(
-                            src_ref=ct_rows.at[:, rows],
-                            dst_ref=cts.at[n, :, rows],
-                            send_sem=ct_send.at[0],
-                            recv_sem=ct_recv.at[n],
-                            device_id=(group, around(1)),
-                            device_id_type=MESH,
+                        remote(
+                            rows, rows, ct_send.at[0], ct_recv.at[n], sibling
                         ).wait_recv()
 
-            last = advance(last, a_64, b_64, 64.0 * KAPPA)
-            last = plus(last, load_rows(cts.at[t], M))
-            store_state(history.at[t + 1], last)
-
-        @pl.when(stage == 0)
-        def _():
-            store_rows(hop_rows, last)
-            for copy in hop:
-                copy.start()
-
-        store_rows(pass_rows, load_state(history.at[local_group + 1]))
+            last = advance(last, a_ref, b_ref, 64.0 * KAPPA)
+            last = plus(last, load_rows(cts.at[t, :, 0 : 8 * m], m))
+            store_state(states.at[t + 1], last)
+        return last
+
+    @pl.when(jnp.logical_and(core0, stage == 0))
+    def _():
+        copy_strip(cts.at[local_group], ct_rows.at[:, :], half_first, HALF_ROWS)
+        begin = load_rows(half_strip, MH)
+        store_state(half_history.at[0], begin)
+        last = chain(begin, a_half, b_half, HALF, half_history, EDGE)
+        store_rows(hop_rows, last)
+        for copy in hop:
+            copy.start()
+        other = (local_group + STAGE // 2) % STAGE
+        for n, t in enumerate((local_group + 1, other, other + 1)):
+            store_rows(pass_rows.at[n], load_state(half_history.at[t]))
+            given[n].start()
+        store_rows(half_strip, load_state(half_history.at[local_group]))
+        for h in range(2):
+            z_in[h, rows_at(half_dst, part)] = half_strip[h, rows_at(half_src, part)]
+
+    @pl.when(jnp.logical_and(core0, stage == 1))
+    def _():
+        store_rows(cts.at[local_group], load_state(ct))
+        for copy in hop_arrivals:
+            copy.wait_recv()
+        begin = load_rows(z_stage, M)
+        store_state(history.at[0], begin)
+        chain(begin, a_64, b_64, CORE, history, HALO)
+        store_rows(pass_rows.at[0], load_state(history.at[local_group + 1]))
         pass_copy.start()
         store_state(z_own, load_state(history.at[local_group]))
 
-    @pl.when(c == 1)
+    @pl.when(stage == 0)
+    def _():
+        half_arrived(1 - mine)
+        pl.when(c == 1)(lambda: half_arrived(mine))
+        store_state(z_own, load_rows(z_in, M))
+
+    @pl.when(jnp.logical_and(c == 1, stage == 1))
     def _():
         pass_copy.wait_recv()
         store_state(z_own, load_rows(z_in, M))
@@ -608,22 +701,23 @@
             pl.when(when)(copy.wait_send)
 
     for halo, when in widths:
-
-        @pl.when(when)
-        def _(halo=halo):
-            copies = ct_copies(halo)
-            for copy in copies[:-1]:
-                copy.wait_send()
-            pl.when(c == 1)(copies[-1].wait_send)
-
-    @pl.when(core0)
+        for of_stage in range(2):
+
+            @pl.when(jnp.logical_and(when, stage == of_stage))
+            def _(halo=halo, of_stage=of_stage):
+                copies = ct_copies(halo, of_stage)
+                for copy in copies[:-1]:
+                    copy.wait_send()
+                pl.when(c == 1)(copies[-1].wait_send)
+
+    @pl.when(jnp.logical_and(core0, stage == 0))
+    def _():
+        for copy in hop + given:
+            copy.wait_send()
+
+    @pl.when(jnp.logical_and(core0, stage == 1))
     def _():
         pass_copy.wait_send()
-
-        @pl.when(stage == 0)
-        def _():
-            for copy in hop:
-                copy.wait_send()
 
 
 def write_out(points, corner, points_out, corner_out, sems):
@@ -668,9 +762,12 @@
         strip_state,
         many(STAGE, 2, ROWS, LANES),
         many(STAGE + 1, 2, M, 8, LANES),
+        many(STAGE + 1, 2, MH, 8, LANES),
+        pltpu.VMEM((2, HALF_ROWS, LANES), F32),
+        *[pltpu.VMEM((2, MH, 8, LANES), F32)] * 2,
+        pltpu.VMEM((2, HALF_ROWS, LANES), F32),
         strip_rows,
-        strip_rows,
-        strip_rows,
+        many(3, 2, ROWS, LANES),
         strip_rows,
         strip_state,
         many(4, 2, ROWS, LANES),
@@ -687,8 +784,8 @@
         dma((STAGE,)),
         dma((4,)),
         dma((4,)),
-        dma,
-        dma,
+        dma((3,)),
+        dma((2,)),
         dma((4,)),
         dma((4,)),
     ]

time: 46.1 us -> 43.7 us (0.948)
  Pallas kernels: 45.1 us -> 42.9 us
    pallas_call x1, Pallas kernels: 44.3 us -> 42.1 us  [local(): pl.pallas_call(kernel, out_shape=(jax.ShapeDtypeStruct((N, N), F32), jax....]
where the time goes in v4:
time: 43.7 us; the launch traced here: 43.6 us
  Pallas kernels  42.9 us (98%)
  between operations  0.64 us (1%)
    pallas_call x1, Pallas kernels, local(): pl.pallas_call(kernel, out_shape=(jax.ShapeDtypeStruct((N, N), F32), jax....  42.1 us

profile of v4, /device:TPU:5, one launch (start us, length us, event | category | flops | bytes accessed | tf_op | source)
XLA Modules:
  0.0 43.6 jit_solution(15741450548801222424)
XLA Ops:
  0.6 42.1 %shard_map.50 = (f32[256,256]{1,0:T(8,128)S(1)}, f32[256,256]{1,0:T(8,128)S(1)}) custom-call(f32[256,256]{1,0:T(8,128)} %init_ref.1, f32[256,256]{1,0:T(8,128)} %rate_ref.1, f32[1,256,256]{2,1,0:T(8,128)} %guess_ref.1), custom_call_target="tpu_custom_call" | custom-call | tf_op jit(solution)/shard_map/pallas_call | solution.py:793
  42.8 0.8 %shard_map.51 = (f32[1,256,256]{2,1,0:T(8,128)}, f32[1,256,256]{2,1,0:T(8,128)}) custom-call(f32[256,256]{1,0:T(8,128)S(1)} %get-tuple-element.4.points, f32[256,256]{1,0:T(8,128)S(1)} %get-tuple-element.5.corner), custom_call_target="tpu_custom_call" | custom-call | tf_op jit(solution)/shard_map/pallas_call | solution.py:807

commit v5 on v4

--- a/solution.py
+++ b/solution.py
@@ -42,8 +42,10 @@
     rest = values - high.astype(F32)
     middle = rest.astype(jnp.bfloat16)
     low = (rest - middle.astype(F32)).astype(jnp.bfloat16)
-    dot = functools.partial(jnp.dot, preferred_element_type=F32)
-    return (dot(high, matrix) + dot(middle, matrix)) + dot(low, matrix)
+    parts = jnp.concatenate([high, middle, low], axis=0)
+    moved = jnp.dot(parts, matrix, preferred_element_type=F32)
+    rows = values.shape[0]
+    return (moved[:rows] + moved[rows : 2 * rows]) + moved[2 * rows :]
 
 
 def advance(state, a_ref, b_ref, scale):
@@ -278,12 +280,16 @@
     slot = (member + 1) % 4
     target = group + (member == 3).astype(jnp.int32)
     have = jnp.logical_or(member < 3, group < groups - 1)
-    for d, part, low, high in (
-        (1, 0, CORE, ROWS),
-        (3, 0, 0, ROWS - CORE),
-        (1, 1, 0, CORE),
-        (3, 1, ROWS - CORE, ROWS),
-        (0, 0, 0, ROWS),
+    for n, (d, part, low, high) in enumerate(
+        (
+            (1, 0, 64, 104),
+            (3, 0, 40, 80),
+            (1, 1, 104, ROWS),
+            (3, 1, 0, 40),
+            (1, 2, 0, 64),
+            (3, 2, 80, ROWS),
+            (0, 0, 0, ROWS),
+        )
     ):
         q = around(d)
         copy = pltpu.make_async_remote_copy(
@@ -291,7 +297,7 @@
                 :, pl.ds(pl.multiple_of(q * CORE + low, 8), high - low)
             ],
             dst_ref=starts.at[slot, :, low:high],
-            send_sem=start_send.at[2 * d + part if d else 0],
+            send_sem=start_send.at[n],
             recv_sem=start_recv.at[slot, part],
             device_id=(target, q),
             device_id_type=MESH,
@@ -351,20 +357,20 @@
             device_id_type=MESH,
         ).wait_recv()
 
-    def make_terms(slots):
+    def make_terms(slots, unroll=8):
         for s in slots:
             start = load_rows(starts.at[s], M)
             store_state(terms.at[s], advance(start, a_16, b_16, 16.0 * KAPPA))
 
         def turn(_, carried):
-            for _ in range(8):
+            for _ in range(unroll):
                 carried = [advance(state, a_1, b_1, KAPPA) for state in carried]
             return tuple(tuple(tuple(half) for half in state) for state in carried)
 
         carried = tuple(
             tuple(tuple(half) for half in load_rows(starts.at[s], M)) for s in slots
         )
-        fine = lax.fori_loop(0, STEPS // 8, turn, carried)
+        fine = lax.fori_loop(0, STEPS // unroll, turn, carried)
         for s, state in zip(slots, fine):
             store_state(terms.at[s], minus(state, load_state(terms.at[s])))
 
@@ -377,14 +383,16 @@
     def _():
         make_terms([slot])
 
-    half = ROWS // 2
-    for s, part, low, to, to_low, d in (
-        (below, 0, CORE, 0, 0, 1),
-        (above, 0, 8, 1, half, 3),
-    ):
+    pieces = (
+        (below, 0, 64, 104, 64, 40, 0, 0, 1),
+        (above, 0, 40, 80, 40, 40, 104, 1, 3),
+        (below, 1, 104, ROWS, 104, 32, 40, 2, 1),
+        (above, 1, 0, 40, 8, 32, 72, 3, 3),
+    )
+    for s, part, low, high, src, count, dst, to, d in pieces:
         copy = pltpu.make_async_remote_copy(
-            src_ref=starts.at[s, :, low : low + half],
-            dst_ref=starts.at[s, :, to_low : to_low + half],
+            src_ref=starts.at[s, :, src : src + count],
+            dst_ref=starts.at[s, :, dst : dst + count],
             send_sem=forward_send.at[to],
             recv_sem=start_recv.at[s, to],
             device_id=(group, around(d)),
@@ -392,8 +400,8 @@
         )
 
         @pl.when(there(s))
-        def _(s=s, d=d, copy=copy):
-            arrived(s, *((CORE, ROWS) if d == 1 else (0, ROWS - CORE)), 0)
+        def _(s=s, part=part, low=low, high=high, copy=copy):
+            arrived(s, low, high, part)
             copy.start()
 
         pending.append((there(s), copy))
@@ -408,20 +416,20 @@
 
     @pl.when(there(below))
     def _():
-        arrived(below, 0, CORE, 1)
+        arrived(below, 0, 64, 2)
 
     @pl.when(there(above))
     def _():
-        arrived(above, ROWS - CORE, ROWS, 1)
+        arrived(above, 80, ROWS, 2)
 
     make_terms([below, above])
 
     @pl.when(there(far))
     def _():
-        arrived(far, 0, half, 0)
-        arrived(far, half, ROWS, 1)
-
-    make_terms([far])
+        for first_row, count, n in ((0, 40, 0), (104, 40, 1), (40, 32, 2), (72, 32, 3)):
+            arrived(far, first_row, first_row + count, n)
+
+    make_terms([far], 16)
 
     def big_step(state, index):
         stepped = advance(state, a_16, b_16, 16.0 * KAPPA)
@@ -495,7 +503,7 @@
     widths = (
         (24, local_group == 0),
         (16, jnp.logical_and(local_group > 0, local_group <= 8)),
-        (8, local_group > 8),
+        (8, jnp.logical_and(local_group > 8, group < groups - 1)),
     )
     for halo, when in widths:
         for of_stage in range(2):
@@ -598,12 +606,12 @@
             there_rows, there_rows, pass_send.at[0], pass_recv.at[which], group
         ).wait_recv()
 
-    def chain(begin, a_ref, b_ref, core, states, edge):
+    def chain(begin, a_ref, b_ref, core, states, edge, steps):
         last = begin
         m = len(begin[0])
-        for t in range(STAGE):
+        for t in range(steps):
             if t % 4 == 0:
-                for n in range(t, t + 4):
+                for n in range(t, min(t + 4, steps)):
                     halo = 24 if n == 0 else 16 if n <= 8 else 8
                     rows = cts.at[n, :, edge - halo : edge + core + halo]
 
@@ -623,7 +631,7 @@
         copy_strip(cts.at[local_group], ct_rows.at[:, :], half_first, HALF_ROWS)
         begin = load_rows(half_strip, MH)
         store_state(half_history.at[0], begin)
-        last = chain(begin, a_half, b_half, HALF, half_history, EDGE)
+        last = chain(begin, a_half, b_half, HALF, half_history, EDGE, STAGE)
         store_rows(hop_rows, last)
         for copy in hop:
             copy.start()
@@ -642,7 +650,7 @@
             copy.wait_recv()
         begin = load_rows(z_stage, M)
         store_state(history.at[0], begin)
-        chain(begin, a_64, b_64, CORE, history, HALO)
+        chain(begin, a_64, b_64, CORE, history, HALO, STAGE - 1)
         store_rows(pass_rows.at[0], load_state(history.at[local_group + 1]))
         pass_copy.start()
         store_state(z_own, load_state(history.at[local_group]))
@@ -774,8 +782,8 @@
         full_rows,
         dma((3,)),
         dma((8,)),
-        dma((4, 2)),
-        dma((2,)),
+        dma((4, 4)),
+        dma((4,)),
         dma((3,)),
         dma((4,)),
         dma((2,)),

time: 43.7 us -> 43.1 us (0.986)
  Pallas kernels: 42.9 us -> 41.9 us
    pallas_call x1, Pallas kernels: 42.1 us -> 41.1 us  [local(): pl.pallas_call(kernel, out_shape=(jax.ShapeDtypeStruct((N, N), F32), jax....]
where the time goes in v5:
time: 43.1 us; the launch traced here: 42.6 us
  Pallas kernels  41.9 us (97%)
  between operations  0.64 us (1%)
    pallas_call x1, Pallas kernels, local(): pl.pallas_call(kernel, out_shape=(jax.ShapeDtypeStruct((N, N), F32), jax....  41.1 us

profile of v5, /device:TPU:5, one launch (start us, length us, event | category | flops | bytes accessed | tf_op | source)
XLA Modules:
  0.0 42.6 jit_solution(12850546368367050248)
XLA Ops:
  0.6 41.1 %shard_map.50 = (f32[256,256]{1,0:T(8,128)S(1)}, f32[256,256]{1,0:T(8,128)S(1)}) custom-call(f32[256,256]{1,0:T(8,128)} %init_ref.1, f32[256,256]{1,0:T(8,128)} %rate_ref.1, f32[1,256,256]{2,1,0:T(8,128)} %guess_ref.1), custom_call_target="tpu_custom_call" | custom-call | tf_op jit(solution)/shard_map/pallas_call | solution.py:801
  41.8 0.8 %shard_map.51 = (f32[1,256,256]{2,1,0:T(8,128)}, f32[1,256,256]{2,1,0:T(8,128)}) custom-call(f32[256,256]{1,0:T(8,128)S(1)} %get-tuple-element.4.points, f32[256,256]{1,0:T(8,128)S(1)} %get-tuple-element.5.corner), custom_call_target="tpu_custom_call" | custom-call | tf_op jit(solution)/shard_map/pallas_call | solution.py:815

commit v6 on v5

--- a/solution.py
+++ b/solution.py
@@ -674,17 +674,18 @@
             state = big_step(state, index)
         store_rows(point_rows.at[index], state if index < 3 else final)
 
+    for d in (2, 1, 3):
+        index = around(d)
         copy = pltpu.make_async_remote_copy(
             src_ref=point_rows.at[index, :, core_rows],
             dst_ref=points_full.at[:, own_rows],
-            send_sem=point_send.at[index],
+            send_sem=point_send.at[d],
             recv_sem=point_recv.at[member],
             device_id=(group, index),
             device_id_type=MESH,
         )
-        when = member != index
-        pl.when(when)(copy.start)
-        pending.append((when, copy))
+        copy.start()
+        pending.append((None, copy))
     for h in range(2):
         points_full[h, own_rows] = point_rows[member, h, core_rows]
     for d in (0, 1, 3, 2):

time: 43.1 us -> 43 us (level)
  no operation moved by 1% of the time
where the time goes in v6:
time: 43 us; the launch traced here: 42.6 us
  Pallas kernels  41.9 us (97%)
  between operations  0.64 us (1%)
    pallas_call x1, Pallas kernels, local(): pl.pallas_call(kernel, out_shape=(jax.ShapeDtypeStruct((N, N), F32), jax....  41.1 us

profile of v6, /device:TPU:5, one launch (start us, length us, event | category | flops | bytes accessed | tf_op | source)
XLA Modules:
  0.0 42.6 jit_solution(10417560471810105042)
XLA Ops:
  0.6 41.1 %shard_map.50 = (f32[256,256]{1,0:T(8,128)S(1)}, f32[256,256]{1,0:T(8,128)S(1)}) custom-call(f32[256,256]{1,0:T(8,128)} %init_ref.1, f32[256,256]{1,0:T(8,128)} %rate_ref.1, f32[1,256,256]{2,1,0:T(8,128)} %guess_ref.1), custom_call_target="tpu_custom_call" | custom-call | tf_op jit(solution)/shard_map/pallas_call | solution.py:802
  41.8 0.8 %shard_map.51 = (f32[1,256,256]{2,1,0:T(8,128)}, f32[1,256,256]{2,1,0:T(8,128)}) custom-call(f32[256,256]{1,0:T(8,128)S(1)} %get-tuple-element.4.points, f32[256,256]{1,0:T(8,128)S(1)} %get-tuple-element.5.corner), custom_call_target="tpu_custom_call" | custom-call | tf_op jit(solution)/shard_map/pallas_call | solution.py:816
